TPU v7x, 32 devices: a whole 2x2x4 slice. The times are simulated.
32 devices in a mesh: tm: 8 (over z, y), table: 4 (over x, core).
Axes of the slice: x: 2, y: 2, z: 4, core: 2. Of those that a mesh axis runs over, the one named last changes fastest.
Arguments:
- item_owner: int32 [8, 6144, 1], P('table', 'tm'), may hold values from 0 to 31; in each aligned block of 768 rows (0 to 767, 768 to 1535, ..., all dimensions but the last counted through in order) at most 48 rows name the same one
- item_row: int32 [8, 6144], P('table', 'tm'), may hold values from 0 to 4095
- history_len: int32 [8], P('table'), may hold values from 1536 to 6144, as said below
- event_gap: float32 [8, 6144], P('table', 'tm'), may hold values from 0 to 18432, as said below
- item_table: bfloat16 [131072, 512], P(('tm', 'table')), may hold values from -6 to 6
- norm_gain: float32 [512], replicated, may hold values from 0.1 to 1.9
- in_weight: bfloat16 [512, 2192], replicated, may hold values from -0.25 to 0.25
- conv_weight: float32 [4, 1152], replicated, may hold values from -3 to 3
- conv_bias: float32 [1152], replicated, may hold values from -3 to 3
- dt_bias: float32 [16], replicated, may hold values from -1 to 1
- decay_rate: float32 [16], replicated, may hold values from 0 to 16, as said below
- out_gain: float32 [1024], replicated, may hold values from 0.1 to 1.9
- emitted_projection: bfloat16 [1024, 512], replicated, may hold values from -0.1875 to 0.1875
Outputs:
- layer_out: bfloat16 [8, 6144, 512], P('table', 'tm')
Inputs may be any that keep to these rules, and one draw needn't show every extreme that they name: `item_owner`: in every user's 768 events held by one device no owner is named more than 48 times, a bound that some block reaches. `history_len`: some user has all 6144 events and some user 6144 // 4. `event_gap`: Positive. `decay_rate`: Positive.
All inputs are finite; a program needn't handle non-finite values.
Results may differ from a plain program's by a relative error of at most 0.01.
Values may be sent and summed in bfloat16 or wider, within the bound.
A program may use at most 192 MiB of HBM per device.

v0:
```python
import jax
import jax.numpy as jnp
from jax import lax
from jax.sharding import PartitionSpec as P

BLOCK = 256


def passed_along(block, axis, distance):
    devices = range(lax.axis_size(axis))
    route = [(i - distance, i) for i in devices if i - distance in devices]
    return lax.ppermute(block, axis, route)


def entering_2(shard, axis, combine, identity):
    length, here = (lax.axis_size(axis), lax.axis_index(axis))
    everything = jax.tree.map(
        lambda part, kind: lax.all_gather(part.astype(kind), axis),
        shard,
        (jnp.bfloat16, jnp.bfloat16),
    )
    start = jax.tree.map(
        lambda part, zero: jnp.broadcast_to(jnp.asarray(zero, part.dtype), part.shape),
        shard,
        identity,
    )

    def hop(k, before):
        reached = k < here
        new = combine(
            before, jax.tree.map(lambda part, own: part[k].astype(own.dtype), everything, shard)
        )
        return jax.tree.map(lambda a, b: jnp.where(reached, a, b), new, before)

    return lax.fori_loop(0, length, hop, start)


def within_blocks(packed):
    streams, in_coef, out_coef, steps, log_decay = packed
    block_len = streams.shape[-1]
    cum_decay = jnp.cumsum(log_decay, axis=2)
    scores = jnp.einsum("cqn,csn->cqs", out_coef, in_coef, preferred_element_type=jnp.float32)
    forward_only = jnp.arange(block_len)[:, None] >= jnp.arange(block_len)[None, :]
    spread = cum_decay[:, :, :, None] - cum_decay[:, :, None, :]
    fading = jnp.exp(jnp.where(forward_only, spread, 0.0))
    mixing = jnp.where(forward_only, scores[:, None] * fading * steps[:, :, None, :], 0.0).astype(
        jnp.bfloat16
    )
    local_y = jnp.einsum("chqs,chps->chpq", mixing, streams, preferred_element_type=jnp.float32)
    to_end = jnp.exp(cum_decay[:, :, -1:] - cum_decay) * steps
    scaled = (to_end[:, :, None, :] * streams.astype(jnp.float32)).astype(jnp.bfloat16)
    block_state = jnp.einsum("chpq,cqn->chpn", scaled, in_coef, preferred_element_type=jnp.float32)
    return (local_y, block_state, cum_decay)


def chain_step(earlier, later):
    return (earlier[0] + later[0], jnp.exp(later[0])[..., None, None] * earlier[1] + later[1])


def head_major(values, user_count, block_count, head_count, head_dim):
    return values.reshape(user_count, block_count, BLOCK, head_count, head_dim).transpose(
        0, 1, 3, 4, 2
    )


def per_device(
    item_owner,
    item_row,
    history_len,
    event_gap,
    item_table,
    norm_gain,
    in_weight,
    conv_weight,
    conv_bias,
    dt_bias,
    decay_rate,
    out_gain,
    emitted_projection,
):
    user_count, events = item_row.shape
    model_dim = item_table.shape[1]
    head_count = dt_bias.shape[0]
    inner_dim = emitted_projection.shape[0]
    head_dim = inner_dim // head_count
    conv_dim = conv_weight.shape[1]
    state_dim = (conv_dim - inner_dim) // 2
    time_count = lax.axis_size("tm")
    devices = time_count * lax.axis_size("table")
    capacity = max(2 * events // devices, 2)
    block_count = events // BLOCK
    owners = item_owner[..., 0]
    owner_match = owners[..., None] == jnp.arange(devices, dtype=jnp.int32)
    owner_hot = owner_match.astype(jnp.bfloat16)
    earlier_mask = (jnp.arange(events)[:, None] > jnp.arange(events)[None, :]).astype(jnp.bfloat16)
    earlier_counts = jnp.einsum(
        "ts,usd->utd", earlier_mask, owner_hot, preferred_element_type=jnp.float32
    )
    slots = jnp.sum(jnp.where(owner_match, earlier_counts, 0.0), axis=-1).astype(jnp.int32)
    user_index = jnp.broadcast_to(
        jnp.arange(user_count, dtype=jnp.int32)[:, None], (user_count, events)
    )
    requests = (
        jnp.zeros((devices, user_count, capacity), jnp.int32)
        .at[owners, user_index, slots]
        .set(item_row)
    )
    fetched = lax.all_to_all(
        jnp.take(
            item_table,
            lax.all_to_all(requests, ("tm", "table"), split_axis=0, concat_axis=0, tiled=True),
            axis=0,
        ),
        ("tm", "table"),
        split_axis=0,
        concat_axis=0,
        tiled=True,
    )
    flat_rows = fetched.reshape(devices * user_count * capacity, model_dim)
    row_place = (owners * user_count + user_index) * capacity + slots
    item_vec = jnp.take(flat_rows, row_place, axis=0)
    item_wide = item_vec.astype(jnp.float32)
    normed = (
        item_wide
        * lax.rsqrt(jnp.mean(item_wide * item_wide, axis=-1, keepdims=True) + 1e-05)
        * norm_gain
    ).astype(jnp.bfloat16)
    projected = jnp.dot(
        normed.reshape(user_count * events, model_dim),
        in_weight,
        preferred_element_type=jnp.float32,
    )
    projected = projected.astype(jnp.bfloat16).reshape(user_count, events, -1)
    conv_in = projected[:, :, inner_dim : inner_dim + conv_dim]
    edge_rows = passed_along(conv_in[:, events - 3 :, :], "tm", 1)
    padded = jnp.concatenate([edge_rows, conv_in], axis=1).astype(jnp.float32)
    conv_sum = conv_bias + conv_weight[0] * padded[:, 0:events]
    for tap_index in range(1, 4):
        conv_sum = conv_sum + conv_weight[tap_index] * padded[:, tap_index : tap_index + events]
    conv_out = jax.nn.silu(conv_sum).astype(jnp.bfloat16)
    streams = head_major(conv_out[:, :, :inner_dim], user_count, block_count, head_count, head_dim)
    in_coef = conv_out[:, :, inner_dim : inner_dim + state_dim].reshape(
        user_count, block_count, BLOCK, state_dim
    )
    out_coef = conv_out[:, :, inner_dim + state_dim :].reshape(
        user_count, block_count, BLOCK, state_dim
    )
    positions = lax.axis_index("tm") * events + jnp.arange(events, dtype=jnp.int32)
    alive = (positions[None, :] < history_len[:, None]).astype(jnp.float32)
    raw_step_size = jnp.swapaxes(projected[:, :, inner_dim + conv_dim :].astype(jnp.float32), 1, 2)
    steps = alive[:, None, :] * jax.nn.softplus(raw_step_size + dt_bias[:, None])
    log_decay = -decay_rate[:, None] * event_gap[:, None, :] * steps
    block_steps = steps.reshape(user_count, head_count, block_count, BLOCK).transpose(0, 2, 1, 3)
    block_decay = log_decay.reshape(user_count, head_count, block_count, BLOCK).transpose(
        0, 2, 1, 3
    )
    local_y, block_state, cum_decay = lax.map(
        within_blocks, (streams, in_coef, out_coef, block_steps, block_decay)
    )
    group_decay = cum_decay[:, :, :, -1]
    running = jnp.zeros((user_count, head_count, head_dim, state_dim), jnp.float32)
    entering = []
    for block_index in range(block_count):
        entering.append(running)
        running = (
            jnp.exp(group_decay[:, block_index])[..., None, None] * running
            + block_state[:, block_index]
        )
    total_decay = jnp.sum(group_decay, axis=1)
    identity = (jnp.zeros_like(total_decay), jnp.zeros_like(running))
    before_decay, incoming = entering_2((total_decay, running), "tm", chain_step, identity)
    prefix_decay = jnp.concatenate(
        [jnp.zeros_like(group_decay[:, :1]), jnp.cumsum(group_decay[:, :-1], axis=1)], axis=1
    )
    held_state = (
        jnp.stack(entering, axis=1) + jnp.exp(prefix_decay)[..., None, None] * incoming[:, None]
    ).astype(jnp.bfloat16)
    carried_y = jnp.exp(cum_decay)[:, :, :, None, :] * jnp.einsum(
        "ucqn,uchpn->uchpq", out_coef, held_state, preferred_element_type=jnp.float32
    )
    response = local_y + carried_y
    gate_raw = head_major(
        projected[:, :, :inner_dim], user_count, block_count, head_count, head_dim
    ).astype(jnp.float32)
    gated = response * jax.nn.silu(gate_raw)
    gated = gated * lax.rsqrt(jnp.mean(gated * gated, axis=3, keepdims=True) + 1e-05)
    normed_y = (gated * out_gain.reshape(head_count, head_dim)[:, :, None]).astype(jnp.bfloat16)
    mixed_out = jnp.einsum(
        "uchpq,hpd->ucqd",
        normed_y,
        emitted_projection.reshape(head_count, head_dim, model_dim),
        preferred_element_type=jnp.float32,
    )
    layer_out = item_wide + mixed_out.reshape(user_count, events, model_dim)
    return (alive[..., None] * layer_out).astype(jnp.bfloat16)


def solution(mesh):
    in_specs = (
        P("table", "tm", None),
        P("table", "tm"),
        P("table"),
        P("table", "tm"),
        P(("tm", "table"), None),
        P(),
        P(),
        P(),
        P(),
        P(),
        P(),
        P(),
        P(),
    )
    out_specs = P("table", "tm", None)
    return jax.shard_map(
        per_device, mesh=mesh, in_specs=in_specs, out_specs=out_specs, check_vma=False
    )
```

profile of v0, /device:TPU:26, one launch (start us, length us, event | category | flops | bytes accessed | tf_op | source)
XLA Modules:
  0.0 321.5 jit_solution(13414650385205044243)
XLA Ops:
  6.5 0.8 copy.131
  7.4 0.4 fusion.52
  7.8 0.7 compare_select_fusion.2
  8.5 0.8 multiply_reduce_fusion.1
  9.3 0.8 and_reduce_fusion
  10.1 0.7 reshape.361
  10.8 6.2 %scatter_custom_fusion = s32[3072]{0:T(1024)S(1)} fusion(s32[1536]{0:T(1024)S(1)} %reshape.359, s32[1536]{0:T(1024)S(1)} %reshape.361, s32[]{:T(128)} %constant.110.clone.1), kind=kCustom, calls=%fused_computation.123 | custom fusion | bytes 12292
  17.1 8.9 %all_to_all.10 = s32[32,2,48]{2,1,0:T(2,128)S(1)} all-to-all(s32[32,2,48]{2,1,0:T(2,128)S(1)} %reshape.340), channel_id=1, replica_groups=mesh['tm'=8,'table'=4] {'tm','table'}, dimensions={0} | all-to-all | bytes 24576 | tf_op jit(solution)/shard_map/all_to_all | solution.py:111
  26.1 16.0 %gather_fusion = bf16[3072,512]{1,0:T(8,128)(2,1)} fusion(bf16[4096,512]{1,0:T(8,128)(2,1)} %param.21, s32[3072]{0:T(1024)S(1)} %broadcast_clamp_fusion), kind=kCustom, calls=%fused_computation | custom fusion | bytes 6303744 | tf_op jit(solution)/shard_map/jit(_take)/gather | solution.py:109
  42.2 3.3 %broadcast_select_fusion = bf16[32,2,48,512]{3,2,1,0:T(8,128)(2,1)} fusion(bf16[32,2,48,512]{3,2,1,0:T(8,128)(2,1)} %bitcast.186, pred[32,2,48]{2,1,0:T(4,128)(4,1)S(1)} %compare_and_fusion), kind=kLoop, calls=%fused_computation.72 | loop fusion | flops 1572864 | bytes 6294528 | tf_op jit(solution)/shard_map/jit(_take)/select_n | solution.py:109
  45.5 7.6 %all-to-all-start.1 = ((bf16[32,2,48,512]{3,2,1,0:T(8,128)(2,1)}), bf16[32,2,48,512]{3,2,1,0:T(8,128)(2,1)}, u32[]{:S(2)}, u32[]{:S(2)}) async-start(bf16[32,2,48,512]{3,2,1,0:T(8,128)(2,1)} %broadcast_select_fusion), calls=%async_computation.1 | async-start | bytes 6291456 | tf_op jit(solution)/shard_map/all_to_all | solution.py:108
  53.6 68.8 %all-to-all-done.1 = bf16[32,2,48,512]{3,2,1,0:T(8,128)(2,1)} async-done(((bf16[32,2,48,512]{3,2,1,0:T(8,128)(2,1)}), bf16[32,2,48,512]{3,2,1,0:T(8,128)(2,1)}, u32[]{:S(2)}, u32[]{:S(2)}) %all-to-all-start.1) | async-done | bytes 3145760 | tf_op jit(solution)/shard_map/all_to_all | solution.py:108
  122.4 7.8 %gather_fusion.1 = bf16[1536,512]{1,0:T(8,128)(2,1)} fusion(bf16[3072,512]{1,0:T(8,128)(2,1)} %bitcast.11, s32[2048]{0:T(1024)S(1)} %pad_clamp_fusion), kind=kCustom, calls=%fused_computation.1 | custom fusion | bytes 3151872 | tf_op jit(solution)/shard_map/jit(_take)/gather | solution.py:121
  130.2 2.1 fusion.33
  132.4 8.1 %convolution_convert_fusion = bf16[1536,2192]{0,1:T(8,128)(2,1)} fusion(bf16[512,2192]{0,1:T(8,128)(2,1)S(1)} %copy-done, f32[512]{0:T(512)S(1)} %copy-done.18, f32[1536]{0:T(1024)S(1)} %rsqrt.20, bf16[1536,512]{1,0:T(8,128)(2,1)} %gather_fusion.1, pred[1536]{0:T(1024)(128)(4,1)S(1)} %broadcast_in_dim.120), kind=kOutput, calls=%fused_computation.43 | convolution fusion | flops 3455016960 | bytes 10561024 | tf_op jit(solution)/shard_map/dot_general | solution.py:128
  140.4 14.5 %reshape.330 = bf16[2,768,2192]{1,0,2:T(2,128)(2,1)} reshape(bf16[1536,2192]{0,1:T(8,128)(2,1)} %convolution_convert_fusion) | data formatting | bytes 13467648 | tf_op jit(solution)/shard_map/reshape | solution.py:133
  154.9 1.8 slice.109
  156.7 0.8 slice.118
  157.5 0.6 copy.94
  158.1 3.9 %collective-permute-start = (bf16[2,3,1152]{2,0,1:T(2,128)(2,1)S(1)}, bf16[2,3,1152]{2,0,1:T(2,128)(2,1)S(1)}, u32[]{:S(2)}, u32[]{:S(2)}) collective-permute-start(bf16[2,3,1152]{2,0,1:T(2,128)(2,1)S(1)} %copy.94), channel_id=1, source_target_pairs={{0,4},{4,8},{8,12},{12,16},{16,20},{20,24},{24,28},{1,5},{5,9},{9,... | collective-permute-start | bytes 41480 | tf_op jit(solution)/shard_map/ppermute | solution.py:12
  162.2 2.0 slice-done
  164.2 2.2 copy.95
  166.6 0.4 copy.69
  167.0 4.0 %maximum_convert_fusion = f32[2,771,1152]{1,2,0:T(8,128)S(1)} fusion(bf16[2,768,1152]{1,2,0:T(8,128)(2,1)} %copy.95, bf16[2,3,1152]{1,2,0:T(8,128)(2,1)S(1)} %copy.69), kind=kLoop, calls=%fused_computation.61 | loop fusion | flops 7105536 | bytes 10658304 | tf_op jit(solution)/shard_map/convert_element_type | solution.py:136
  170.9 6.8 %multiply_convert_fusion.4 = bf16[2,768,1152]{1,2,0:T(8,128)(2,1)S(1)} fusion(f32[2,771,1152]{1,2,0:T(8,128)S(1)} %maximum_convert_fusion, f32[1152]{0:T(1024)S(1)} %get-tuple-element.208, f32[1152]{0:T(1024)S(1)} %get-tuple-element.209, f32[1152]{0:T(1024)S(1)} %get-tuple-element.207, f32[1152]{0:T(1024)S(1)} %get-tuple-element.206, f32[1152]{0:T(1024)S(1)} %copy-done.12), kind=kLoop, calls=%fused_computation.52 | loop fusion | flops 23003136 | bytes 31873536 | tf_op jit(solution)/shard_map/convert_element_type | solution.py:140
  177.8 1.9 slice.115
  179.7 9.4 %reshape.331 = bf16[2,3,256,16,64]{2,1,4,3,0:T(4,128)(2,1)} reshape(bf16[2,768,1024]{1,2,0:T(8,128)(2,1)} %slice.115) | data formatting | bytes 6291456 | tf_op jit(solution)/shard_map/reshape | solution.py:61
  189.0 4.5 %copy.71 = bf16[2,3,16,64,256]{4,3,2,1,0:T(8,128)(2,1)} copy(bf16[2,3,16,64,256]{4,1,3,2,0:T(4,128)(2,1)} %bitcast.185) | data formatting | bytes 6291456 | tf_op jit(solution)/shard_map/while | solution.py:157
  193.6 22.6 %while.28 = (s32[]{:T(128)}, f32[2,3,16,64,256]{4,3,2,1,0:T(8,128)}, f32[2,3,16,64,64]{4,3,2,0,1:T(8,128)}, f32[2,3,16,256]{3,2,1,0:T(8,128)S(1)}, bf16[2,3,16,6...) while((s32[]{:T(128)}, ...), condition=%wide.region_6.7_spmd, body=%wide.region_3.6_spmd.sunk | while | flops 551403648 | bytes 36314964 | solution.py:157
  193.7 1.7 reduce-window.12
  195.4 0.2 slice_reduce_fusion.9
  196.0 0.3 fusion.99
  196.3 6.1 %bitcast_dynamic-update-slice_fusion.4 = f32[2,3,16,64,256]{4,3,2,1,0:T(8,128)} fusion(f32[2,3,16,64,256]{4,3,2,1,0:T(8,128)} %get-tuple-element.360, s32[]{:T(128)} %get-tuple-element.359, f32[3,16,256]{2,1,0:T(8,128)S(1)} %get-tuple-element.341, f32[3,16,256]{2,1,0:T(8,128)S(1)} %copy_bitcast_fusion.6, f32[3,256,256]{2,1,0:T(8,128)S(1)} %fusion.99, ...), kind=kOutput, calls=%fused_computation.14.clone.1 | convolution fusion | flops 421527552 | bytes 5719040 | tf_op jit(solution)/shard_map/while/body/eval_jaxpr/chqs,chps->chpq/dot_general | solution.py:49
  202.5 0.6 bitcast_dynamic-update-slice_fusion.5
  203.1 1.6 copy-done.4
  204.9 1.7 reduce-window.12
  206.7 0.2 slice_reduce_fusion.9
  207.2 0.3 fusion.99
  207.6 6.2 %bitcast_dynamic-update-slice_fusion.4 = f32[2,3,16,64,256]{4,3,2,1,0:T(8,128)} fusion(f32[2,3,16,64,256]{4,3,2,1,0:T(8,128)} %get-tuple-element.360, s32[]{:T(128)} %get-tuple-element.359, f32[3,16,256]{2,1,0:T(8,128)S(1)} %get-tuple-element.341, f32[3,16,256]{2,1,0:T(8,128)S(1)} %copy_bitcast_fusion.6, f32[3,256,256]{2,1,0:T(8,128)S(1)} %fusion.99, ...), kind=kOutput, calls=%fused_computation.14.clone.1 | convolution fusion | flops 421527552 | bytes 5719040 | tf_op jit(solution)/shard_map/while/body/eval_jaxpr/chqs,chps->chpq/dot_general | solution.py:49
  213.8 0.6 bitcast_dynamic-update-slice_fusion.5
  214.4 1.6 copy-done.4
  216.2 0.2 slice_reduce_fusion.6
  216.5 3.1 fusion.55
  219.6 1.9 slice-done.1
  221.5 3.1 copy_convert_fusion
  224.6 10.7 %reshape.342 = f32[2,3,256,16,64]{2,1,4,3,0:T(4,128)} reshape(f32[2,768,1024]{1,2,0:T(8,128)} %copy_convert_fusion) | data formatting | bytes 12582912 | tf_op jit(solution)/shard_map/convert_element_type | solution.py:184
  235.4 14.8 %all-gather.1 = bf16[8,2,16]{2,1,0:T(2,128)(2,1)S(1)} all-gather(bf16[1,2,16]{2,1,0:T(2,128)(2,1)S(1)} %bitcast.202), channel_id=2, replica_groups=mesh['tm'=8,'table'=4] {'tm'}, dimensions={0}, use_global_device_ids=true | all-gather | bytes 576 | tf_op jit(solution)/shard_map/all_gather | solution.py:18
  250.3 1.8 multiply_add_fusion
  252.1 39.3 %all-gather.4.cloned.1.call-done = bf16[8,2,16,64,64]{4,3,2,1,0:T(8,128)(2,1)} async-done(((bf16[1,2,16,64,64]{4,3,2,1,0:T(8,128)(2,1)}), bf16[8,2,16,64,64]{4,3,2,1,0:T(8,128)(2,1)}) %all-gather.4.cloned.1.call-update) | async-done | bytes 2097168 | tf_op jit(solution)/shard_map/all_gather | solution.py:18
  291.4 10.7 %while.29 = (s32[]{:T(128)}, f32[2,16,64,64]{3,2,1,0:T(8,128)S(1)}, s32[]{:T(128)}, bf16[8,2,16]{2,1,0:T(2,128)(2,1)S(1)}, bf16[8,2,16,64,64]{4,3,2,1,0:T(8,128)(2,1)}, /*index=5*/s32[]{:T(128)}, s32[]{:T(128)}) while((s32[]{:T(128)}, f32[2,16,64,64]{3,2,1,0:T(8,128)S(1)}, s32[]{:T(128)}, bf16[8,2,16]{2,1,0:T(2,128)(2,1)S(1)}, ...), condition=%wide.region_10.11_spmd.clone, body=%wide.region_9.10_spmd.clone.sunk | while | flops 655396 | bytes 1311145 | solution.py:35
  291.4 1.3 fusion.100
  292.7 1.3 fusion.100
  294.0 1.3 fusion.100
  295.4 1.3 fusion.100
  296.7 1.3 fusion.100
  298.1 1.3 fusion.100
  299.4 1.3 fusion.100
  300.7 1.3 fusion.100
  302.1 6.9 %multiply_reduce_fusion = (f32[2,3,16,256]{3,2,1,0:T(8,128)S(1)}, f32[2,3,16,64,256]{4,3,2,1,0:T(8,128)S(1)}) fusion(f32[2,3,256,16,64]{2,1,4,3,0:T(4,128)} %reshape.342, f32[2,3,16,64,256]{4,3,2,1,0:T(8,128)} %get-tuple-element.148, bf16[2,3,256,64,1]{2,1,3,0,4:T(4,128)(2,1)S(1)} %bitcast.196, f32[2,3,16,256]{3,2,1,0:T(8,128)S(1)} %exp.72, ...), kind=kOutput, calls=%fused_computation.60 | convolution fusion | flops 217423872 | bytes 20840844 | tf_op jit(solution)/shard_map/ucqn,uchpn->uchpq/dot_general | solution.py:178
  309.0 0.9 fusion.36
  310.0 0.3 copy.107
  310.3 1.1 copy-done.5
  311.4 0.3 copy-done.17
  311.7 2.9 fusion.35
  (123 shorter events, 2.7 us)
Async XLA Ops:
  6.5 125.8 %copy-start = (bf16[512,2192]{0,1:T(8,128)(2,1)S(1)}, bf16[512,2192]{0,1:T(8,128)(2,1)}, u32[]{:S(2)}) copy-start(bf16[512,2192]{0,1:T(8,128)(2,1)} %param.23) | copy-start | bytes 6733828
  45.5 7.7 %copy-start.6 = (s32[2,768,1]{1,2,0:T(1,128)S(1)}, s32[2,768,1]{1,2,0:T(1,128)}, u32[]{:S(2)}) copy-start(s32[2,768,1]{1,2,0:T(1,128)} %param.17) | copy-start | bytes 18436
  45.5 7.9 %copy-start.19 = (f32[16]{0:T(128)S(1)}, f32[16]{0:T(128)}, u32[]{:S(2)}) copy-start(f32[16]{0:T(128)} %param.27) | copy-start | bytes 196
  45.5 7.9 %copy-start.9 = (f32[4,1152]{1,0:T(4,128)S(1)}, f32[4,1152]{1,0:T(4,128)}, u32[]{:S(2)}) copy-start(f32[4,1152]{1,0:T(4,128)} %param.24) | copy-start | bytes 55300
  45.5 8.0 %copy-start.16 = (s32[2]{0:T(128)S(1)}, s32[2]{0:T(128)}, u32[]{:S(2)}) copy-start(s32[2]{0:T(128)} %param.19) | copy-start | bytes 28
  45.5 76.9 %all-to-all-start.1 = ((bf16[32,2,48,512]{3,2,1,0:T(8,128)(2,1)}), bf16[32,2,48,512]{3,2,1,0:T(8,128)(2,1)}, u32[]{:S(2)}, u32[]{:S(2)}) async-start(bf16[32,2,48,512]{3,2,1,0:T(8,128)(2,1)} %broadcast_select_fusion), calls=%async_computation.1 | async-start | bytes 6291456 | tf_op jit(solution)/shard_map/all_to_all | solution.py:108
  53.1 238.2 %all-gather.4.cloned.1.call-start = ((), (), s32[]{:S(2)}) async-start(), calls=%async_computation.2 | async-start | bytes 4718592 | tf_op jit(solution)/shard_map/all_gather | solution.py:18
  53.4 76.9 %copy-start.10 = (pred[2,768,1]{1,0,2:T(4,128)(4,1)}, pred[2,768,1]{1,0,2:T(4,128)(4,1)S(1)}, u32[]{:S(2)}) copy-start(pred[2,768,1]{1,0,2:T(4,128)(4,1)S(1)} %copy.130) | copy-start | bytes 4612
  53.6 108.4 %copy-start.7 = (f32[2,768]{1,0:T(2,128)}, f32[2,768]{1,0:T(2,128)S(1)}, u32[]{:S(2)}) copy-start(f32[2,768]{1,0:T(2,128)S(1)} %compare_convert_fusion) | copy-start | bytes 18436
  122.4 9.9 %copy-start.18 = (f32[512]{0:T(512)S(1)}, f32[512]{0:T(512)}, u32[]{:S(2)}) copy-start(f32[512]{0:T(512)} %param.22) | copy-start | bytes 6148
  140.4 21.6 %copy-start.13 = (f32[2,768]{1,0:T(2,128)S(1)}, f32[2,768]{1,0:T(2,128)}, u32[]{:S(2)}) copy-start(f32[2,768]{1,0:T(2,128)} %param.20) | copy-start | bytes 18436
  140.4 21.6 %copy-start.15 = (f32[16]{0:T(128)S(1)}, f32[16]{0:T(128)}, u32[]{:S(2)}) copy-start(f32[16]{0:T(128)} %param.26) | copy-start | bytes 196
  158.1 8.5 %collective-permute-start = (bf16[2,3,1152]{2,0,1:T(2,128)(2,1)S(1)}, bf16[2,3,1152]{2,0,1:T(2,128)(2,1)S(1)}, u32[]{:S(2)}, u32[]{:S(2)}) collective-permute-start(bf16[2,3,1152]{2,0,1:T(2,128)(2,1)S(1)} %copy.94), channel_id=1, source_target_pairs={{0,4},{4,8},{8,12},{12,16},{16,20},{20,24},{24,28},{1,5},{5,9},{9,... | collective-permute-start | bytes 41480 | tf_op jit(solution)/shard_map/ppermute | solution.py:12
  162.2 2.0 slice-start
  167.0 4.0 %copy-start.12 = (f32[1152]{0:T(1024)S(1)}, f32[1152]{0:T(1024)}, u32[]{:S(2)}) copy-start(f32[1152]{0:T(1024)} %param.25) | copy-start | bytes 13828
  196.3 6.2 %copy-start.2 = (bf16[2,3,16,64,256]{4,3,2,1,0:T(8,128)(2,1)S(1)}, bf16[2,3,16,64,256]{4,3,2,1,0:T(8,128)(2,1)}, u32[]{:S(2)}) copy-start(bf16[2,3,16,64,256]{4,3,2,1,0:T(8,128)(2,1)} %get-tuple-element.374) | copy-start | bytes 9437188 | tf_op jit(solution)/shard_map/while
  196.3 6.1 %copy-start.3 = (f32[2,3,16,64,64]{4,3,2,0,1:T(8,128)S(1)}, f32[2,3,16,64,64]{4,3,2,0,1:T(8,128)}, u32[]{:S(2)}) copy-start(f32[2,3,16,64,64]{4,3,2,0,1:T(8,128)} %get-tuple-element.361) | copy-start | bytes 4718596 | tf_op jit(solution)/shard_map/while
  203.0 1.7 copy-start.4
  207.6 6.2 %copy-start.2 = (bf16[2,3,16,64,256]{4,3,2,1,0:T(8,128)(2,1)S(1)}, bf16[2,3,16,64,256]{4,3,2,1,0:T(8,128)(2,1)}, u32[]{:S(2)}) copy-start(bf16[2,3,16,64,256]{4,3,2,1,0:T(8,128)(2,1)} %get-tuple-element.374) | copy-start | bytes 9437188 | tf_op jit(solution)/shard_map/while
  207.6 6.2 %copy-start.3 = (f32[2,3,16,64,64]{4,3,2,0,1:T(8,128)S(1)}, f32[2,3,16,64,64]{4,3,2,0,1:T(8,128)}, u32[]{:S(2)}) copy-start(f32[2,3,16,64,64]{4,3,2,0,1:T(8,128)} %get-tuple-element.361) | copy-start | bytes 4718596 | tf_op jit(solution)/shard_map/while
  214.3 1.7 copy-start.4
  216.2 3.4 %copy-start.14 = (f32[1024]{0:T(1024)S(1)}, f32[1024]{0:T(1024)}, u32[]{:S(2)}) copy-start(f32[1024]{0:T(1024)} %param.28) | copy-start | bytes 12292
  219.6 1.9 slice-start.1
  310.0 1.4 copy-start.5
  310.0 1.4 copy-start.8
  310.0 1.4 copy-start.11
  310.0 1.7 copy-start.17
  311.7 2.9 copy-start.1
Sparse Core Ops, SparseCore 0:
  219.7 71.6 all-gather.3
where the time goes:
time: 327 us; the launch traced here: 321 us
  waiting for transfers between devices  108 us (33%)
  local copies, waits for them, and re-layouts  88.9 us (27%)
  other arithmetic  42.4 us (13%)
  matrix products  32.4 us (10%)
  blocking collectives  23.7 us (7%)
  between operations  13.9 us (4%)
  starting transfers between devices  11.5 us (4%)
    all_to_all x1, waiting for transfers between devices, per_device(): lax.all_to_all(jnp.take(item_table, lax.all_to_all(requests, ('tm', 'tabl...  68.8 us
    all_gather x1, waiting for transfers between devices, entering_2(): lax.all_gather(part.astype(kind), axis)  39.3 us
    gather x1, local copies, waits for them, and re-layouts, per_device(): jnp.take(item_table, lax.all_to_all(requests, ('tm', 'table'), split_axis...  16 us
    all_gather x1, blocking collectives, entering_2(): lax.all_gather(part.astype(kind), axis)  14.8 us
    reshape x1, local copies, waits for them, and re-layouts, per_device(): projected = projected.astype(jnp.bfloat16).reshape(user_count, events, -1)  14.5 us
    dot_general x2, matrix products, within_blocks(): jnp.einsum('chqs,chps->chpq', mixing, streams, preferred_element_type=jnp...  12.3 us
    unnamed x41, local copies, waits for them, and re-layouts  12 us
    convert_element_type x1, local copies, waits for them, and re-layouts, per_device(): gate_raw = head_major(projected[:, :, :inner_dim], user_count, block_coun...  10.7 us
  transfers between devices with their start and end apart: 3, of which 2 were waited for; matrix products, arithmetic and copies ran while one was open for 6% of the time, Pallas kernels for 0%

commit v1 on v0

v1 whole, which is shorter than its diff:
```python
import jax
import jax.numpy as jnp
from jax import lax
from jax.experimental import pallas as pl
from jax.experimental.pallas import tpu as pltpu
from jax.sharding import PartitionSpec as P

BLOCK = 256
F32 = jnp.float32
BF16 = jnp.bfloat16
VMEM_LIMIT = 40 * 1024 * 1024


def passed_along(block, axis, distance):
    devices = range(lax.axis_size(axis))
    route = [(i - distance, i) for i in devices if i - distance in devices]
    return lax.ppermute(block, axis, route)


def head_spread(head_count, inner_dim):
    head_dim = inner_dim // head_count
    lane = lax.broadcasted_iota(jnp.int32, (head_count, inner_dim), 1)
    row = lax.broadcasted_iota(jnp.int32, (head_count, inner_dim), 0)
    first = row * head_dim
    return jnp.where((lane >= first) & (lane < first + head_dim), 1.0, 0.0).astype(BF16)


def over_channels(values, spread):
    high = values.astype(BF16)
    low = (values - high.astype(F32)).astype(BF16)
    return jnp.dot(high, spread, preferred_element_type=F32) + jnp.dot(
        low, spread, preferred_element_type=F32
    )


def silu(v):
    return v / (1.0 + jnp.exp(-v))


def project_kernel(inner_dim, conv_dim, place, rows, gain, weight, item, gate, conv, step):
    count = rows.shape[0]
    lane = lax.broadcasted_iota(jnp.int32, (BLOCK, count), 1)
    hot = jnp.where(lane == place[...], 1.0, 0.0).astype(BF16)
    wide = jnp.dot(hot, rows[...], preferred_element_type=F32)
    item[...] = wide.astype(BF16)
    scale = lax.rsqrt(jnp.mean(wide * wide, axis=-1, keepdims=True) + 1e-05)
    normed = (wide * scale * gain[...]).astype(BF16)
    gate[...] = jnp.dot(normed, weight[:, :inner_dim], preferred_element_type=F32).astype(BF16)
    conv[...] = jnp.dot(
        normed, weight[:, inner_dim : inner_dim + conv_dim], preferred_element_type=F32
    ).astype(BF16)
    step[...] = (
        jnp.dot(normed, weight[:, inner_dim + conv_dim :], preferred_element_type=F32)
        .astype(BF16)
        .astype(F32)
    )


def state_kernel(
    inner_dim, conv, step, gap, alive, edge, taps, bias, dt_bias, rate,
    x_out, bc_out, steps_out, cum_out, entering, before, final, factor,
    padded, running, gone,
):
    head_count = step.shape[1]
    state_dim = entering.shape[1]
    block_index = pl.program_id(0)

    @pl.when(block_index == 0)
    def _():
        padded[0:8] = edge[...].astype(F32)
        running[...] = jnp.zeros_like(running)
        gone[...] = jnp.zeros_like(gone)

    padded[8 : 8 + BLOCK] = conv[...].astype(F32)
    total = bias[...] + taps[0:1] * padded[5 : 5 + BLOCK]
    for k in range(1, 4):
        total = total + taps[k : k + 1] * padded[5 + k : 5 + k + BLOCK]
    padded[0:8] = padded[BLOCK : BLOCK + 8]
    out = silu(total).astype(BF16)
    x = out[:, :inner_dim]
    bc = out[:, inner_dim:]
    x_out[...] = x
    bc_out[...] = bc
    raw = step[...] + dt_bias[...]
    soft = jnp.maximum(raw, 0.0) + jnp.log1p(jnp.exp(-jnp.abs(raw)))
    steps = alive[...] * soft
    log_decay = -rate[...] * gap[...] * steps
    below = lax.broadcasted_iota(jnp.int32, (BLOCK, BLOCK), 0) >= lax.broadcasted_iota(
        jnp.int32, (BLOCK, BLOCK), 1
    )
    cum = jnp.dot(
        jnp.where(below, 1.0, 0.0), log_decay, preferred_element_type=F32,
        precision=lax.Precision.HIGHEST,
    )
    steps_out[...] = steps
    cum_out[...] = cum
    last = cum[BLOCK - 1 : BLOCK]
    spread = head_spread(head_count, inner_dim)
    scaled = (over_channels(jnp.exp(last - cum) * steps, spread) * x.astype(F32)).astype(BF16)
    block_state = lax.dot_general(
        bc[:, :state_dim], scaled, (((0,), (0,)), ((), ())), preferred_element_type=F32
    )
    entering[0] = running[...]
    before[0] = over_channels(jnp.exp(gone[...]), spread)
    fade = over_channels(jnp.broadcast_to(jnp.exp(last), gone.shape), spread)
    new = fade[0:1] * running[...] + block_state
    running[...] = new
    gone[...] = gone[...] + last
    final[...] = new
    factor[...] = over_channels(jnp.exp(gone[...]), spread)


def local_kernel(x, bc, steps, cum, y):
    head_count = steps.shape[1]
    inner_dim = x.shape[1]
    state_dim = bc.shape[1] // 2
    spread = head_spread(head_count, inner_dim)
    xs = (over_channels(steps[...], spread) * x[...].astype(F32)).astype(BF16)
    scores = lax.dot_general(
        bc[:, state_dim:], bc[:, :state_dim], (((1,), (1,)), ((), ())),
        preferred_element_type=F32,
    )
    below = lax.broadcasted_iota(jnp.int32, (BLOCK, BLOCK), 0) >= lax.broadcasted_iota(
        jnp.int32, (BLOCK, BLOCK), 1
    )
    scores = jnp.where(below, scores, 0.0)
    down = cum[...]
    across = down.T
    width = 2 * (inner_dim // head_count)
    left = lax.broadcasted_iota(jnp.int32, (BLOCK, width), 1) < width // 2
    for pair in range(head_count // 2):
        lanes = slice(pair * width, (pair + 1) * width)
        parts = []
        for h in (2 * pair, 2 * pair + 1):
            fading = jnp.exp(jnp.minimum(down[:, h : h + 1] - across[h : h + 1], 0.0))
            mixing = (scores * fading).astype(BF16)
            parts.append(jnp.dot(mixing, xs[:, lanes], preferred_element_type=F32))
        y[:, lanes] = jnp.where(left, parts[0], parts[1])


def emit_kernel(
    y, bc, cum, gate, item, alive, entering, before, incoming, gain, weight, out
):
    head_count = cum.shape[1]
    inner_dim = y.shape[1]
    state_dim = bc.shape[1] // 2
    spread = head_spread(head_count, inner_dim)
    held = (entering[0] + before[0, 0:1] * incoming[...]).astype(BF16)
    carried = jnp.dot(bc[:, state_dim:], held, preferred_element_type=F32)
    response = y[...] + over_channels(jnp.exp(cum[...]), spread) * carried
    gated = response * silu(gate[...].astype(F32))
    squares = lax.dot_general(
        (gated * gated).astype(BF16), spread, (((1,), (1,)), ((), ())),
        preferred_element_type=F32,
    )
    scale = lax.rsqrt(squares * (head_count / inner_dim) + 1e-05)
    normed = (gated * over_channels(scale, spread) * gain[...]).astype(BF16)
    mixed = jnp.dot(normed, weight[...], preferred_element_type=F32)
    out[...] = (alive[...] * (item[...].astype(F32) + mixed)).astype(BF16)


def rows_of(width):
    return pl.BlockSpec((BLOCK, width), lambda i: (i, 0))


def whole(*shape):
    return pl.BlockSpec(shape, lambda i: (0,) * len(shape))


def one_of(*shape):
    return pl.BlockSpec((1, *shape), lambda i: (i,) + (0,) * len(shape))


def params():
    return pltpu.CompilerParams(
        vmem_limit_bytes=VMEM_LIMIT, dimension_semantics=("arbitrary",)
    )


def cost(flops, size, exps=0):
    return pl.CostEstimate(flops=flops, bytes_accessed=size, transcendentals=exps)


def struct(shape, dtype):
    return jax.ShapeDtypeStruct(shape, dtype)


def earlier_spans(state, factor):
    length, here = (lax.axis_size("tm"), lax.axis_index("tm"))
    size = state.shape[0]
    total, fade = (jnp.zeros_like(state), jnp.ones_like(factor))
    distance = 1
    while distance < length:
        own = state + factor * total
        own_fade = factor * fade
        high = own_fade.astype(BF16)
        low = (own_fade - high.astype(F32)).astype(BF16)
        packed = jnp.concatenate([own.astype(BF16), high, low], axis=0)
        got = passed_along(packed, "tm", distance).astype(F32)
        reached = here >= distance
        got_fade = jnp.where(reached, got[size : size + 1] + got[size + 1 : size + 2], 1.0)
        total = total + fade * got[:size]
        fade = fade * got_fade
        distance *= 2
    return total


def per_device(
    item_owner,
    item_row,
    history_len,
    event_gap,
    item_table,
    norm_gain,
    in_weight,
    conv_weight,
    conv_bias,
    dt_bias,
    decay_rate,
    out_gain,
    emitted_projection,
):
    user_count, events = item_row.shape
    model_dim = item_table.shape[1]
    head_count = dt_bias.shape[0]
    inner_dim = emitted_projection.shape[0]
    conv_dim = conv_weight.shape[1]
    state_dim = (conv_dim - inner_dim) // 2
    projected_dim = in_weight.shape[1]
    devices = lax.axis_size("tm") * lax.axis_size("table")
    capacity = max(2 * events // devices, 2)
    blocks = events // BLOCK
    slots_all = devices * capacity

    owners = item_owner[..., 0]
    owner_match = owners[..., None] == jnp.arange(devices, dtype=jnp.int32)
    owner_hot = owner_match.astype(BF16)
    earlier_mask = (jnp.arange(events)[:, None] > jnp.arange(events)[None, :]).astype(BF16)
    earlier_counts = jnp.einsum(
        "ts,usd->utd", earlier_mask, owner_hot, preferred_element_type=F32
    )
    slots = jnp.sum(jnp.where(owner_match, earlier_counts, 0.0), axis=-1).astype(jnp.int32)
    slot_match = slots[..., None] == jnp.arange(capacity, dtype=jnp.int32)
    row_high = item_row // 64
    row_low = item_row - row_high * 64
    parts = jnp.concatenate(
        [
            jnp.where(slot_match, row_high[..., None], 0),
            jnp.where(slot_match, row_low[..., None], 0),
        ],
        axis=-1,
    ).astype(BF16)
    asked = jnp.einsum("utd,utc->duc", owner_hot, parts, preferred_element_type=F32)
    requests = (64.0 * asked[..., :capacity] + asked[..., capacity:]).astype(jnp.int32)
    wanted = lax.all_to_all(requests, ("tm", "table"), split_axis=0, concat_axis=0, tiled=True)
    place = owners * capacity + slots

    positions = lax.axis_index("tm") * events + jnp.arange(events, dtype=jnp.int32)
    alive = (positions[None, :] < history_len[:, None]).astype(F32)

    fetched = []
    for user in range(user_count):
        sent = jnp.take(item_table, wanted[:, user].reshape(-1), axis=0, mode="clip")
        fetched.append(
            lax.all_to_all(
                sent.reshape(devices, capacity, model_dim),
                ("tm", "table"),
                split_axis=0,
                concat_axis=0,
                tiled=True,
            ).reshape(slots_all, model_dim)
        )

    outputs = []
    for user in range(user_count):
        alive_column = alive[user][:, None]
        item, gate, conv, step = pl.pallas_call(
            lambda *refs: project_kernel(inner_dim, conv_dim, *refs),
            grid=(blocks,),
            in_specs=[
                rows_of(1),
                whole(slots_all, model_dim),
                whole(1, model_dim),
                whole(model_dim, projected_dim),
            ],
            out_specs=[rows_of(model_dim), rows_of(inner_dim), rows_of(conv_dim), rows_of(head_count)],
            out_shape=[
                struct((events, model_dim), BF16),
                struct((events, inner_dim), BF16),
                struct((events, conv_dim), BF16),
                struct((events, head_count), F32),
            ],
            compiler_params=params(),
            cost_estimate=cost(2 * events * model_dim * (projected_dim + slots_all), 9 << 20),
            name="project",
        )(place[user][:, None], fetched[user], norm_gain[None], in_weight)
        edge = passed_along(conv[events - 8 :], "tm", 1)
        x, bc, steps, cum, entering, before, final, factor = pl.pallas_call(
            lambda *refs: state_kernel(inner_dim, *refs),
            grid=(blocks,),
            in_specs=[
                rows_of(conv_dim),
                rows_of(head_count),
                rows_of(1),
                rows_of(1),
                whole(8, conv_dim),
                whole(4, conv_dim),
                whole(1, conv_dim),
                whole(1, head_count),
                whole(1, head_count),
            ],
            out_specs=[
                rows_of(inner_dim),
                rows_of(2 * state_dim),
                rows_of(head_count),
                rows_of(head_count),
                one_of(state_dim, inner_dim),
                one_of(8, inner_dim),
                whole(state_dim, inner_dim),
                whole(8, inner_dim),
            ],
            out_shape=[
                struct((events, inner_dim), BF16),
                struct((events, 2 * state_dim), BF16),
                struct((events, head_count), F32),
                struct((events, head_count), F32),
                struct((blocks, state_dim, inner_dim), F32),
                struct((blocks, 8, inner_dim), F32),
                struct((state_dim, inner_dim), F32),
                struct((8, inner_dim), F32),
            ],
            scratch_shapes=[
                pltpu.VMEM((BLOCK + 8, conv_dim), F32),
                pltpu.VMEM((state_dim, inner_dim), F32),
                pltpu.VMEM((8, head_count), F32),
            ],
            compiler_params=params(),
            cost_estimate=cost(4 << 30, 8 << 20, events * conv_dim),
            name="states",
        )(
            conv, step, event_gap[user][:, None], alive_column, edge,
            conv_weight, conv_bias[None], dt_bias[None], decay_rate[None],
        )
        incoming = earlier_spans(final, factor[0:1])
        y = pl.pallas_call(
            local_kernel,
            grid=(blocks,),
            in_specs=[
                rows_of(inner_dim), rows_of(2 * state_dim), rows_of(head_count), rows_of(head_count),
            ],
            out_specs=rows_of(inner_dim),
            out_shape=struct((events, inner_dim), F32),
            compiler_params=params(),
            cost_estimate=cost(8 << 30, 5 << 20, events * BLOCK * head_count),
            name="local",
        )(x, bc, steps, cum)
        outputs.append(
            pl.pallas_call(
                emit_kernel,
                grid=(blocks,),
                in_specs=[
                    rows_of(inner_dim),
                    rows_of(2 * state_dim),
                    rows_of(head_count),
                    rows_of(inner_dim),
                    rows_of(model_dim),
                    rows_of(1),
                    one_of(state_dim, inner_dim),
                    one_of(8, inner_dim),
                    whole(state_dim, inner_dim),
                    whole(1, inner_dim),
                    whole(inner_dim, model_dim),
                ],
                out_specs=rows_of(model_dim),
                out_shape=struct((events, model_dim), BF16),
                compiler_params=params(),
                cost_estimate=cost(4 << 30, 9 << 20, events * inner_dim),
                name="emit",
            )(
                y, bc, cum, gate, item, alive_column, entering, before, incoming,
                out_gain[None], emitted_projection,
            )
        )
    return jnp.stack(outputs)


def solution(mesh):
    in_specs = (
        P("table", "tm", None),
        P("table", "tm"),
        P("table"),
        P("table", "tm"),
        P(("tm", "table"), None),
        P(),
        P(),
        P(),
        P(),
        P(),
        P(),
        P(),
        P(),
    )
    out_specs = P("table", "tm", None)
    return jax.shard_map(
        per_device, mesh=mesh, in_specs=in_specs, out_specs=out_specs, check_vma=False
    )
```

time: 327 us -> 182 us (0.56); the launches traced: 321 us -> 181 us
  local copies, waits for them, and re-layouts: 88.9 us -> 32.9 us
  waiting for transfers between devices: 108 us -> 59.5 us
  Pallas kernels: 0 us -> 46.7 us
  other arithmetic: 42.4 us -> 2.93 us
  matrix products: 32.4 us -> 0.56 us
  starting transfers between devices: 11.5 us -> 29.4 us
  blocking collectives: 23.7 us -> 8.92 us
  between operations: 13.9 us -> 0.71 us
    pallas_call x0 -> x8, Pallas kernels: none -> 46.7 us  [the longest x2 16 us: per_device(): pl.pallas_call(lambda *refs: state_kernel(inner_dim, *refs), grid=(blocks...]
    all_gather x1 -> x0, waiting for transfers between devices: 39.3 us -> none  [entering_2(): lax.all_gather(part.astype(kind), axis)]
    dot_general x9 -> x1, matrix products: 32 us -> 0.18 us  [per_device(): jnp.einsum('utd,utc->duc', owner_hot, parts, preferred_element_type=F32)]
    all_to_all x1 -> x2, waiting for transfers between devices: 68.8 us -> 41 us  [per_device(): lax.all_to_all(sent.reshape(devices, capacity, model_dim), ('tm', 'table'...]
    reshape x11 -> x0, local copies, waits for them, and re-layouts: 24.2 us -> none  [the longest x1 14.5 us: per_device(): projected = projected.astype(jnp.bfloat16).reshape(user_count, events, -1)]
    ppermute x1 -> x8, waiting for transfers between devices: 0.01 us -> 18.5 us  [passed_along(): return lax.ppermute(block, axis, route)]
    convert_element_type x5 -> x19, other arithmetic: 17 us -> 0.58 us  [the longest x6 0.23 us: earlier_spans(): packed = jnp.concatenate([own.astype(BF16), high, low], axis=0)]
    all_gather x1 -> x0, blocking collectives: 14.8 us -> none  [entering_2(): lax.all_gather(part.astype(kind), axis)]
  transfers between devices with their start and end apart: 3 -> 10, of which waited for: 2 -> 5; matrix products, arithmetic and copies ran while one was open for 6% -> 9% of each run, Pallas kernels for 0% -> 18%
where the time goes in v1:
time: 182 us; the launch traced here: 181 us
  waiting for transfers between devices  59.5 us (33%)
  Pallas kernels  46.7 us (26%)
  local copies, waits for them, and re-layouts  32.9 us (18%)
  starting transfers between devices  29.4 us (16%)
  blocking collectives  8.92 us (5%)
  other arithmetic  2.93 us (2%)
    all_to_all x2, waiting for transfers between devices, per_device(): lax.all_to_all(sent.reshape(devices, capacity, model_dim), ('tm', 'table'...  41 us
    ppermute x8, waiting for transfers between devices, passed_along(): return lax.ppermute(block, axis, route)  18.5 us
    ppermute x8, starting transfers between devices, passed_along(): return lax.ppermute(block, axis, route)  16.5 us
    gather x2, local copies, waits for them, and re-layouts, per_device(): jnp.take(item_table, wanted[:, user].reshape(-1), axis=0, mode='clip')  16.4 us
    pallas_call x2, Pallas kernels, per_device(): pl.pallas_call(lambda *refs: state_kernel(inner_dim, *refs), grid=(blocks...  16 us
    all_to_all x2, starting transfers between devices, per_device(): lax.all_to_all(sent.reshape(devices, capacity, model_dim), ('tm', 'table'...  12.9 us
    unnamed x48, local copies, waits for them, and re-layouts  12.1 us
    pallas_call x2, Pallas kernels, per_device(): pl.pallas_call(emit_kernel, grid=(blocks,), in_specs=[rows_of(inner_dim),...  11.8 us
  transfers between devices with their start and end apart: 10, of which 5 were waited for; matrix products, arithmetic and copies ran while one was open for 9% of the time, Pallas kernels for 18%

profile of v1, /device:TPU:26, one launch (start us, length us, event | category | flops | bytes accessed | tf_op | source)
XLA Modules:
  0.0 181.5 jit_solution(4036914071264301941)
XLA Ops:
  0.0 0.7 copy.41
  0.7 0.4 fusion.9
  1.1 0.7 multiply_subtract_fusion
  1.9 0.2 convolution_bitcast_fusion
  2.0 0.1 fusion.19
  2.2 8.9 %all_to_all.15 = s32[32,2,48]{2,1,0:T(2,128)S(1)} all-to-all(s32[32,2,48]{2,1,0:T(2,128)S(1)} %copy.26), channel_id=1, replica_groups=mesh['tm'=8,'table'=4] {'tm','table'}, dimensions={0} | all-to-all | bytes 24576 | tf_op jit(solution)/shard_map/all_to_all | solution.py:255
  11.1 0.1 slice_reduce_fusion.1
  11.2 0.1 reshape.30
  11.3 8.2 %gather_fusion = bf16[1536,512]{1,0:T(8,128)(2,1)} fusion(bf16[4096,512]{1,0:T(8,128)(2,1)} %param.17, s32[2048]{0:T(1024)S(1)} %pad_clamp_fusion.1), kind=kCustom, calls=%fused_computation | custom fusion | bytes 3151872 | tf_op jit(solution)/shard_map/jit(_take)/gather | solution.py:263
  19.5 6.7 %all-to-all-start.1 = ((bf16[32,48,512]{2,1,0:T(8,128)(2,1)}), bf16[32,48,512]{2,1,0:T(8,128)(2,1)S(1)}, u32[]{:S(2)}, u32[]{:S(2)}) async-start(bf16[32,48,512]{2,1,0:T(8,128)(2,1)} %bitcast.62), calls=%async_computation.1 | async-start | bytes 3145728 | tf_op jit(solution)/shard_map/all_to_all | solution.py:265
  26.2 0.1 reshape.38
  26.3 8.2 %gather_fusion.1 = bf16[1536,512]{1,0:T(8,128)(2,1)} fusion(bf16[4096,512]{1,0:T(8,128)(2,1)} %param.17, s32[2048]{0:T(1024)S(1)} %pad_clamp_fusion), kind=kCustom, calls=%fused_computation.1 | custom fusion | bytes 3151872 | tf_op jit(solution)/shard_map/jit(_take)/gather | solution.py:263
  34.5 26.9 %all-to-all-done.1 = bf16[32,48,512]{2,1,0:T(8,128)(2,1)S(1)} async-done(((bf16[32,48,512]{2,1,0:T(8,128)(2,1)}), bf16[32,48,512]{2,1,0:T(8,128)(2,1)S(1)}, u32[]{:S(2)}, u32[]{:S(2)}) %all-to-all-start.1) | async-done | bytes 1572896 | tf_op jit(solution)/shard_map/all_to_all | solution.py:265
  61.5 0.0 copy-start.19
  61.5 1.2 copy-done
  62.6 6.2 %all-to-all-start.2 = ((bf16[32,48,512]{2,1,0:T(8,128)(2,1)}), bf16[32,48,512]{2,1,0:T(8,128)(2,1)}, u32[]{:S(2)}, u32[]{:S(2)}) async-start(bf16[32,48,512]{2,1,0:T(8,128)(2,1)} %bitcast.61), calls=%async_computation.2 | async-start | bytes 3145728 | tf_op jit(solution)/shard_map/all_to_all | solution.py:265
  68.9 0.1 compare_convert_fusion
  69.0 0.2 copy.30.refs_3_.alive
  69.2 0.9 copy.29.refs_2_
  70.2 0.9 copy.27.refs_0_
  71.1 0.2 copy.35.refs_3_.alive
  71.3 0.2 copy.34.refs_2_
  71.5 0.9 copy.32.refs_0_
  72.4 2.8 %copy.28.refs_3_ = bf16[512,2192]{1,0:T(8,128)(2,1)S(1)} copy(bf16[512,2192]{0,1:T(8,128)(2,1)} %param.19) | data formatting | bytes 4489216 | tf_op args[6]
  75.3 1.4 copy-done.1
  76.7 1.0 copy-done.4
  77.7 4.5 %project.2 = (bf16[768,512]{1,0:T(8,128)(2,1)S(1)}, bf16[768,1024]{1,0:T(8,128)(2,1)S(1)}, bf16[768,1152]{1,0:T(8,128)(2,1)S(1)}, f32[768,16]{1,0:T(8,128)S(1)}) custom-call(s32[768,1]{1,0:T(8,128)S(1)} %copy-done.4, bf16[1536,512]{1,0:T(8,128)(2,1)S(1)} %bitcast.50, f32[1,512]{1,0:T(1,128)S(1)} %bitcast.55, bf16[512,2192]{1,0:T(8,128)(2,1)S(1)} %copy.28.refs_3_), custom_call_target="tpu_custom_call" | custom-call | flops 2931818496 | bytes 9437184 | tf_op jit(solution)/shard_map/project/pallas_call | solution.py:277
  82.1 1.2 copy-done.13
  83.3 0.9 copy-done.15
  84.2 0.7 copy-done.17
  84.9 0.6 slice.96
  85.5 1.2 copy-done.5
  86.8 3.4 %collective-permute-start = (bf16[8,1152]{1,0:T(8,128)(2,1)}, bf16[8,1152]{1,0:T(8,128)(2,1)}, u32[]{:S(2)}, u32[]{:S(2)}) collective-permute-start(bf16[8,1152]{1,0:T(8,128)(2,1)} %slice.96), channel_id=1, source_target_pairs={{0,4},{4,8},{8,12},{12,16},{16,20},{20,24},{24,28},{1,5},{5,9},{9,... | collective-permute-start | bytes 55304 | tf_op jit(solution)/shard_map/ppermute | solution.py:17
  90.2 14.1 %all-to-all-done.2 = bf16[32,48,512]{2,1,0:T(8,128)(2,1)} async-done(((bf16[32,48,512]{2,1,0:T(8,128)(2,1)}), bf16[32,48,512]{2,1,0:T(8,128)(2,1)}, u32[]{:S(2)}, u32[]{:S(2)}) %all-to-all-start.2) | async-done | bytes 1572896 | tf_op jit(solution)/shard_map/all_to_all | solution.py:265
  104.2 1.0 copy-done.3
  105.2 0.0 copy-start.12
  105.2 6.1 %project.3 = (bf16[768,512]{1,0:T(8,128)(2,1)S(1)}, bf16[768,1024]{1,0:T(8,128)(2,1)S(1)}, bf16[768,1152]{1,0:T(8,128)(2,1)S(1)}, f32[768,16]{1,0:T(8,128)S(1)}) custom-call(s32[768,1]{1,0:T(8,128)S(1)} %copy-done.3, bf16[1536,512]{1,0:T(8,128)(2,1)} %bitcast.18.refs_1_, f32[1,512]{1,0:T(1,128)S(1)} %bitcast.56, bf16[512,2192]{1,0:T(8,128)(2,1)S(1)} %copy.28.refs_3_), custom_call_target="tpu_custom_call" | custom-call | flops 2931818496 | bytes 9437184 | tf_op jit(solution)/shard_map/project/pallas_call | solution.py:277
  111.3 3.8 %collective-permute-start.4 = (bf16[8,1152]{1,0:T(8,128)(2,1)S(1)}, bf16[8,1152]{1,0:T(8,128)(2,1)S(1)}, u32[]{:S(2)}, u32[]{:S(2)}) collective-permute-start(bf16[8,1152]{1,0:T(8,128)(2,1)S(1)} %slice.110), channel_id=1, source_target_pairs={{0,4},{4,8},{8,12},{12,16},{16,20},{20,24},{24,28},{1,5},{5,9},{9,... | collective-permute-start | bytes 55304 | tf_op jit(solution)/shard_map/ppermute | solution.py:17
  115.1 0.0 collective-permute-done.refs_4_
  115.2 8.3 %states.2 = (bf16[768,1024]{1,0:T(8,128)(2,1)S(1)}, bf16[768,128]{1,0:T(8,128)(2,1)S(1)}, f32[768,16]{1,0:T(8,128)S(1)}, f32[768,16]{1,0:T(8,128)S(1)}, f32[3,64...) custom-call(bf16[768,1152]{1,0:T(8,128)(2,1)S(1)} %copy-done.6, ...), custom_call_target="tpu_custom_call" | custom-call | flops 4294967296 | bytes 8388608 | tf_op jit(solution)/shard_map/states/pallas_call | solution.py:298
  123.6 0.0 collective-permute-done.4.refs_4_
  123.6 7.6 %states.3 = (bf16[768,1024]{1,0:T(8,128)(2,1)S(1)}, bf16[768,128]{1,0:T(8,128)(2,1)S(1)}, f32[768,16]{1,0:T(8,128)S(1)}, f32[768,16]{1,0:T(8,128)S(1)}, f32[3,64...) custom-call(bf16[768,1152]{1,0:T(8,128)(2,1)S(1)} %get-tuple-element.41.refs_0_,, ...), custom_call_target="tpu_custom_call" | custom-call | flops 4294967296 | bytes 8388608 | tf_op jit(solution)/shard_map/states/pallas_call | solution.py:298
  131.3 1.9 %collective-permute-start.1 = (bf16[66,1024]{1,0:T(8,128)(2,1)S(1)}, bf16[66,1024]{1,0:T(8,128)(2,1)S(1)}, u32[]{:S(2)}, u32[]{:S(2)}) collective-permute-start(bf16[66,1024]{1,0:T(8,128)(2,1)S(1)} %pad_maximum_fusion.1), channel_id=1, source_target_pairs={{0,4},{4,8},{8,12},{12,16},{16,20},{20,24},{24,28},{1,5},{5,9},{9,... | collective-permute-start | bytes 405512 | tf_op jit(solution)/shard_map/ppermute | solution.py:17
  133.3 2.1 %collective-permute-start.5 = (bf16[66,1024]{1,0:T(8,128)(2,1)S(1)}, bf16[66,1024]{1,0:T(8,128)(2,1)S(1)}, u32[]{:S(2)}, u32[]{:S(2)}) collective-permute-start(bf16[66,1024]{1,0:T(8,128)(2,1)S(1)} %pad_maximum_fusion.4), channel_id=1, source_target_pairs={{0,4},{4,8},{8,12},{12,16},{16,20},{20,24},{24,28},{1,5},{5,9},{9,... | collective-permute-start | bytes 405512 | tf_op jit(solution)/shard_map/ppermute | solution.py:17
  135.4 4.2 %local.3.y = f32[768,1024]{1,0:T(8,128)S(1)} custom-call(bf16[768,1024]{1,0:T(8,128)(2,1)S(1)} %get-tuple-element.43.x, bf16[768,128]{1,0:T(8,128)(2,1)S(1)} %get-tuple-element.44.bc, f32[768,16]{1,0:T(8,128)S(1)} %get-tuple-element.45.steps, f32[768,16]{1,0:T(8,128)S(1)} %get-tuple-element.46.cum), custom_call_target="tpu_custom_call" | custom-call | flops 8589934592 | bytes 5242880 | tf_op jit(solution)/shard_map/local/pallas_call | solution.py:345
  139.6 4.2 %local.2.y = f32[768,1024]{1,0:T(8,128)S(1)} custom-call(bf16[768,1024]{1,0:T(8,128)(2,1)S(1)} %get-tuple-element.31.x, bf16[768,128]{1,0:T(8,128)(2,1)S(1)} %get-tuple-element.32.bc, f32[768,16]{1,0:T(8,128)S(1)} %get-tuple-element.33.steps, f32[768,16]{1,0:T(8,128)S(1)} %get-tuple-element.34.cum), custom_call_target="tpu_custom_call" | custom-call | flops 8589934592 | bytes 5242880 | tf_op jit(solution)/shard_map/local/pallas_call | solution.py:345
  143.8 0.0 collective-permute-done.1
  143.9 0.0 collective-permute-done.5
  144.1 1.3 collective-permute-start.6
  145.4 1.3 collective-permute-start.2
  146.7 7.2 %collective-permute-done.6 = bf16[66,1024]{1,0:T(8,128)(2,1)S(1)} collective-permute-done((bf16[66,1024]{1,0:T(8,128)(2,1)S(1)}, bf16[66,1024]{1,0:T(8,128)(2,1)S(1)}, u32[]{:S(2)}, u32[]{:S(2)}) %collective-permute-start.6) | collective-permute-done | bytes 135200 | tf_op jit(solution)/shard_map/ppermute | solution.py:17
  153.9 0.1 add_convert_fusion
  154.0 0.0 copy-start.7
  154.0 0.0 copy-start.9
  154.1 1.4 collective-permute-start.7
  155.5 0.3 collective-permute-done.2
  155.8 0.1 add_convert_fusion.3
  155.9 1.3 collective-permute-start.3
  157.2 11.0 %collective-permute-done.7 = bf16[66,1024]{1,0:T(8,128)(2,1)S(1)} collective-permute-done((bf16[66,1024]{1,0:T(8,128)(2,1)S(1)}, bf16[66,1024]{1,0:T(8,128)(2,1)S(1)}, u32[]{:S(2)}, u32[]{:S(2)}) %collective-permute-start.7) | collective-permute-done | bytes 135200 | tf_op jit(solution)/shard_map/ppermute | solution.py:17
  168.2 0.1 multiply_add_fusion.incoming
  168.3 5.9 %emit.3 = bf16[768,512]{1,0:T(8,128)(2,1)S(1)} custom-call(f32[768,1024]{1,0:T(8,128)S(1)} %local.3.y, bf16[768,128]{1,0:T(8,128)(2,1)S(1)} %get-tuple-element.44.bc, f32[768,16]{1,0:T(8,128)S(1)} %get-tuple-element.46.cum, bf16[768,1024]{1,0:T(8,128)(2,1)S(1)} %get-tuple-element.47.gate, bf16[768,512]{1,0:T(8,128)(2,1)S(1)} %get-tuple-element.48.item, ...), custom_call_target="tpu_custom_call" | custom-call | flops 4294967296 | bytes 9437184 | tf_op jit(solution)/shard_map/emit/pallas_call | solution.py:358
  174.2 0.1 multiply_add_fusion.1.incoming
  174.3 5.9 %emit.2 = bf16[768,512]{1,0:T(8,128)(2,1)S(1)} custom-call(f32[768,1024]{1,0:T(8,128)S(1)} %local.2.y, bf16[768,128]{1,0:T(8,128)(2,1)S(1)} %get-tuple-element.32.bc, f32[768,16]{1,0:T(8,128)S(1)} %get-tuple-element.34.cum, bf16[768,1024]{1,0:T(8,128)(2,1)S(1)} %copy-done.14, bf16[768,512]{1,0:T(8,128)(2,1)S(1)} %copy-done.16, ...), custom_call_target="tpu_custom_call" | custom-call | flops 4294967296 | bytes 9437184 | tf_op jit(solution)/shard_map/emit/pallas_call | solution.py:358
  180.2 1.3 pad_maximum_fusion
  (74 shorter events, 0.7 us)
Async XLA Ops:
  19.5 41.9 %all-to-all-start.1 = ((bf16[32,48,512]{2,1,0:T(8,128)(2,1)}), bf16[32,48,512]{2,1,0:T(8,128)(2,1)S(1)}, u32[]{:S(2)}, u32[]{:S(2)}) async-start(bf16[32,48,512]{2,1,0:T(8,128)(2,1)} %bitcast.62), calls=%async_computation.1 | async-start | bytes 3145728 | tf_op jit(solution)/shard_map/all_to_all | solution.py:265
  61.5 1.2 copy-start
  61.5 7.4 %copy-start.20 = (f32[1152]{0:T(1024)S(1)}, f32[1152]{0:T(1024)}, u32[]{:S(2)}) copy-start(f32[1152]{0:T(1024)} %param.21) | copy-start | bytes 13828
  61.5 7.4 %copy-start.22 = (s32[2]{0:T(128)S(1)}, s32[2]{0:T(128)}, u32[]{:S(2)}) copy-start(s32[2]{0:T(128)} %param.15) | copy-start | bytes 28
  61.5 7.7 %copy-start.21 = (f32[2,768]{1,0:T(2,128)S(1)}, f32[2,768]{1,0:T(2,128)}, u32[]{:S(2)}) copy-start(f32[2,768]{1,0:T(2,128)} %param.16) | copy-start | bytes 18436
  61.5 8.7 %copy-start.19 = (s32[2,768,1]{1,2,0:T(1,128)S(1)}, s32[2,768,1]{1,2,0:T(1,128)}, u32[]{:S(2)}) copy-start(s32[2,768,1]{1,2,0:T(1,128)} %param.13) | copy-start | bytes 18436
  62.6 41.6 %all-to-all-start.2 = ((bf16[32,48,512]{2,1,0:T(8,128)(2,1)}), bf16[32,48,512]{2,1,0:T(8,128)(2,1)}, u32[]{:S(2)}, u32[]{:S(2)}) async-start(bf16[32,48,512]{2,1,0:T(8,128)(2,1)} %bitcast.61), calls=%async_computation.2 | async-start | bytes 3145728 | tf_op jit(solution)/shard_map/all_to_all | solution.py:265
  72.4 2.8 %copy-start.10 = (f32[512]{0:T(512)S(1)}, f32[512]{0:T(512)}, u32[]{:S(2)}) copy-start(f32[512]{0:T(512)} %param.18) | copy-start | bytes 6148
  75.2 1.4 copy-start.1
  76.7 1.0 copy-start.4
  82.1 1.2 copy-start.13
  83.3 0.9 copy-start.15
  84.2 0.7 copy-start.17
  85.5 1.2 copy-start.5
  86.8 28.4 %collective-permute-start = (bf16[8,1152]{1,0:T(8,128)(2,1)}, bf16[8,1152]{1,0:T(8,128)(2,1)}, u32[]{:S(2)}, u32[]{:S(2)}) collective-permute-start(bf16[8,1152]{1,0:T(8,128)(2,1)} %slice.96), channel_id=1, source_target_pairs={{0,4},{4,8},{8,12},{12,16},{16,20},{20,24},{24,28},{1,5},{5,9},{9,... | collective-permute-start | bytes 55304 | tf_op jit(solution)/shard_map/ppermute | solution.py:17
  104.2 1.0 copy-start.3
  105.2 9.9 %copy-start.2 = (f32[768,1]{1,0:T(8,128)S(1)}, f32[768,1]{1,0:T(8,128)}, u32[]{:S(2)}) copy-start(f32[768,1]{1,0:T(8,128)} %copy.29.refs_2_) | copy-start | bytes 9220
  105.2 9.9 %copy-start.6 = (bf16[768,1152]{1,0:T(8,128)(2,1)S(1)}, bf16[768,1152]{1,0:T(8,128)(2,1)}, u32[]{:S(2)}) copy-start(bf16[768,1152]{1,0:T(8,128)(2,1)} %copy-done.5) | copy-start | bytes 5308420
  105.2 10.0 %copy-start.8 = (f32[4,1152]{1,0:T(4,128)S(1)}, f32[4,1152]{1,0:T(4,128)}, u32[]{:S(2)}) copy-start(f32[4,1152]{1,0:T(4,128)} %refs_5_.3) | copy-start | bytes 55300
  105.2 10.0 %copy-start.11 = (f32[16]{0:T(128)S(1)}, f32[16]{0:T(128)}, u32[]{:S(2)}) copy-start(f32[16]{0:T(128)} %param.22) | copy-start | bytes 196
  105.2 10.0 %copy-start.12 = (f32[16]{0:T(128)S(1)}, f32[16]{0:T(128)}, u32[]{:S(2)}) copy-start(f32[16]{0:T(128)} %param.23) | copy-start | bytes 196
  105.2 10.0 %copy-start.18 = (f32[768,16]{1,0:T(8,128)S(1)}, f32[768,16]{1,0:T(8,128)}, u32[]{:S(2)}) copy-start(f32[768,16]{1,0:T(8,128)} %copy-done.17) | copy-start | bytes 147460
  111.3 12.3 %collective-permute-start.4 = (bf16[8,1152]{1,0:T(8,128)(2,1)S(1)}, bf16[8,1152]{1,0:T(8,128)(2,1)S(1)}, u32[]{:S(2)}, u32[]{:S(2)}) collective-permute-start(bf16[8,1152]{1,0:T(8,128)(2,1)S(1)} %slice.110), channel_id=1, source_target_pairs={{0,4},{4,8},{8,12},{12,16},{16,20},{20,24},{24,28},{1,5},{5,9},{9,... | collective-permute-start | bytes 55304 | tf_op jit(solution)/shard_map/ppermute | solution.py:17
  131.3 12.5 %collective-permute-start.1 = (bf16[66,1024]{1,0:T(8,128)(2,1)S(1)}, bf16[66,1024]{1,0:T(8,128)(2,1)S(1)}, u32[]{:S(2)}, u32[]{:S(2)}) collective-permute-start(bf16[66,1024]{1,0:T(8,128)(2,1)S(1)} %pad_maximum_fusion.1), channel_id=1, source_target_pairs={{0,4},{4,8},{8,12},{12,16},{16,20},{20,24},{24,28},{1,5},{5,9},{9,... | collective-permute-start | bytes 405512 | tf_op jit(solution)/shard_map/ppermute | solution.py:17
  133.3 10.6 %collective-permute-start.5 = (bf16[66,1024]{1,0:T(8,128)(2,1)S(1)}, bf16[66,1024]{1,0:T(8,128)(2,1)S(1)}, u32[]{:S(2)}, u32[]{:S(2)}) collective-permute-start(bf16[66,1024]{1,0:T(8,128)(2,1)S(1)} %pad_maximum_fusion.4), channel_id=1, source_target_pairs={{0,4},{4,8},{8,12},{12,16},{16,20},{20,24},{24,28},{1,5},{5,9},{9,... | collective-permute-start | bytes 405512 | tf_op jit(solution)/shard_map/ppermute | solution.py:17
  144.1 9.8 %collective-permute-start.6 = (bf16[66,1024]{1,0:T(8,128)(2,1)S(1)}, bf16[66,1024]{1,0:T(8,128)(2,1)S(1)}, u32[]{:S(2)}, u32[]{:S(2)}) collective-permute-start(bf16[66,1024]{1,0:T(8,128)(2,1)S(1)} %pad_maximum_fusion.5), channel_id=1, source_target_pairs={{0,8},{4,12},{8,16},{12,20},{16,24},{20,28},{1,9},{5,13},{9,17},{1... | collective-permute-start | bytes 405512 | tf_op jit(solution)/shard_map/ppermute | solution.py:17
  145.4 10.4 %collective-permute-start.2 = (bf16[66,1024]{1,0:T(8,128)(2,1)S(1)}, bf16[66,1024]{1,0:T(8,128)(2,1)S(1)}, u32[]{:S(2)}, u32[]{:S(2)}) collective-permute-start(bf16[66,1024]{1,0:T(8,128)(2,1)S(1)} %pad_maximum_fusion.2), channel_id=1, source_target_pairs={{0,8},{4,12},{8,16},{12,20},{16,24},{20,28},{1,9},{5,13},{9,17},{1... | collective-permute-start | bytes 405512 | tf_op jit(solution)/shard_map/ppermute | solution.py:17
  154.0 14.3 %copy-start.7 = (bf16[1024,512]{1,0:T(8,128)(2,1)S(1)}, bf16[1024,512]{1,0:T(8,128)(2,1)}, u32[]{:S(2)}) copy-start(bf16[1024,512]{1,0:T(8,128)(2,1)} %weight.3) | copy-start | bytes 3145732
  154.0 14.3 %copy-start.9 = (f32[1024]{0:T(1024)S(1)}, f32[1024]{0:T(1024)}, u32[]{:S(2)}) copy-start(f32[1024]{0:T(1024)} %param.24) | copy-start | bytes 12292
  154.1 14.2 %collective-permute-start.7 = (bf16[66,1024]{1,0:T(8,128)(2,1)S(1)}, bf16[66,1024]{1,0:T(8,128)(2,1)S(1)}, u32[]{:S(2)}, u32[]{:S(2)}) collective-permute-start(bf16[66,1024]{1,0:T(8,128)(2,1)S(1)} %pad_maximum_fusion.6), channel_id=1, source_target_pairs={{0,16},{4,20},{8,24},{12,28},{1,17},{5,21},{9,25},{13,29},{2,18},{... | collective-permute-start | bytes 405512 | tf_op jit(solution)/shard_map/ppermute | solution.py:17
  155.9 18.3 %collective-permute-start.3 = (bf16[66,1024]{1,0:T(8,128)(2,1)S(1)}, bf16[66,1024]{1,0:T(8,128)(2,1)S(1)}, u32[]{:S(2)}, u32[]{:S(2)}) collective-permute-start(bf16[66,1024]{1,0:T(8,128)(2,1)S(1)} %pad_maximum_fusion.3), channel_id=1, source_target_pairs={{0,16},{4,20},{8,24},{12,28},{1,17},{5,21},{9,25},{13,29},{2,18},{... | collective-permute-start | bytes 405512 | tf_op jit(solution)/shard_map/ppermute | solution.py:17
  168.3 6.0 %copy-start.14 = (bf16[768,1024]{1,0:T(8,128)(2,1)S(1)}, bf16[768,1024]{1,0:T(8,128)(2,1)}, u32[]{:S(2)}) copy-start(bf16[768,1024]{1,0:T(8,128)(2,1)} %copy-done.13) | copy-start | bytes 4718596
  168.3 6.0 %copy-start.16 = (bf16[768,512]{1,0:T(8,128)(2,1)S(1)}, bf16[768,512]{1,0:T(8,128)(2,1)}, u32[]{:S(2)}) copy-start(bf16[768,512]{1,0:T(8,128)(2,1)} %copy-done.15) | copy-start | bytes 2359300

commit v2 on v1

--- a/solution.py
+++ b/solution.py
@@ -35,6 +35,107 @@
 
 def silu(v):
     return v / (1.0 + jnp.exp(-v))
+
+
+def exchange_kernel(
+    count, group, requests, table_hbm, fetched,
+    table, asked, wanted, ready, table_sem, self_sem, ask_send, ask_recv, row_send, row_recv,
+):
+    tm, across = (lax.axis_index("tm"), lax.axis_index("table"))
+    width = lax.axis_size("table")
+    me = tm * width + across
+    half = count // 2
+
+    def device(index):
+        return (index // width, index % width)
+
+    def ask(k):
+        target = (me + k) % count
+        return pltpu.make_async_remote_copy(
+            src_ref=requests.at[target],
+            dst_ref=wanted.at[k],
+            send_sem=ask_send.at[k],
+            recv_sem=ask_recv.at[k],
+            device_id=device(target),
+            device_id_type=pl.DeviceIdType.MESH,
+        )
+
+    def give(k):
+        return pltpu.make_async_remote_copy(
+            src_ref=ready.at[:, k],
+            dst_ref=fetched.at[:, k],
+            send_sem=row_send.at[k],
+            recv_sem=row_recv.at[k],
+            device_id=device((me + count - k) % count),
+            device_id_type=pl.DeviceIdType.MESH,
+        )
+
+    asked[...] = jnp.zeros_like(asked)
+    loading = pltpu.make_async_copy(table_hbm, table, table_sem)
+    loading.start()
+    own_ask = pltpu.make_async_copy(requests.at[me], wanted.at[0], self_sem)
+    own_ask.start()
+    barrier = pltpu.get_barrier_semaphore()
+
+    @pl.loop(1, count)
+    def _(k):
+        pl.semaphore_signal(
+            barrier, inc=1, device_id=device((me + k) % count),
+            device_id_type=pl.DeviceIdType.MESH,
+        )
+
+    pl.semaphore_wait(barrier, count - 1)
+
+    def kth(p):
+        return jnp.where(p % 2 == 0, half + p // 2, ((p + 1) // 2) % half)
+
+    @pl.loop(0, count - 1)
+    def _(p):
+        ask(kth(p)).start()
+
+    own_ask.wait()
+    loading.wait()
+    users, _, slots, _ = ready.shape
+    lanes = users * slots
+    rows = table.shape[0]
+
+    @pl.loop(0, count // group)
+    def _(g):
+        for j in range(group):
+            k = kth(g * group + j)
+
+            @pl.when(k != 0)
+            def _():
+                ask(k).wait_recv()
+
+            asked[j : j + 1] = wanted[k].astype(F32)
+        columns = asked[...].T
+        hot = []
+        lane = lax.broadcasted_iota(jnp.int32, (lanes, rows), 1)
+        for j in range(group):
+            column = columns[:lanes, j : j + 1].astype(jnp.int32)
+            hot.append(jnp.where(lane == column, 1.0, 0.0).astype(BF16))
+        found = jnp.dot(jnp.concatenate(hot, axis=0), table[...], preferred_element_type=F32)
+        found = found.astype(BF16)
+        for j in range(group):
+            k = kth(g * group + j)
+            for user in range(users):
+                start = j * lanes + user * slots
+                ready[user, k] = found[start : start + slots]
+
+            @pl.when(k != 0)
+            def _():
+                give(k).start()
+
+    own = pltpu.make_async_copy(ready.at[:, 0], fetched.at[:, 0], self_sem)
+    own.start()
+
+    @pl.loop(1, count)
+    def _(k):
+        ask(k).wait_send()
+        give(k).wait()
+
+    own.wait()
 
 
 def project_kernel(inner_dim, conv_dim, place, rows, gain, weight, item, gate, conv, step):
@@ -63,7 +164,7 @@
 ):
     head_count = step.shape[1]
     state_dim = entering.shape[1]
-    block_index = pl.program_id(0)
+    block_index = pl.program_id(1)
 
     @pl.when(block_index == 0)
     def _():
@@ -160,20 +261,24 @@
 
 
 def rows_of(width):
-    return pl.BlockSpec((BLOCK, width), lambda i: (i, 0))
+    return pl.BlockSpec((None, BLOCK, width), lambda u, i: (u, i, 0))
 
 
 def whole(*shape):
-    return pl.BlockSpec(shape, lambda i: (0,) * len(shape))
+    return pl.BlockSpec(shape, lambda u, i: (0,) * len(shape))
+
+
+def user_of(*shape):
+    return pl.BlockSpec((None, *shape), lambda u, i: (u,) + (0,) * len(shape))
 
 
 def one_of(*shape):
-    return pl.BlockSpec((1, *shape), lambda i: (i,) + (0,) * len(shape))
+    return pl.BlockSpec((None, 1, *shape), lambda u, i: (u, i) + (0,) * len(shape))
 
 
 def params():
     return pltpu.CompilerParams(
-        vmem_limit_bytes=VMEM_LIMIT, dimension_semantics=("arbitrary",)
+        vmem_limit_bytes=VMEM_LIMIT, dimension_semantics=("arbitrary", "arbitrary")
     )
 
 
@@ -187,7 +292,7 @@
 
 def earlier_spans(state, factor):
     length, here = (lax.axis_size("tm"), lax.axis_index("tm"))
-    size = state.shape[0]
+    size = state.shape[1]
     total, fade = (jnp.zeros_like(state), jnp.ones_like(factor))
     distance = 1
     while distance < length:
@@ -195,11 +300,11 @@
         own_fade = factor * fade
         high = own_fade.astype(BF16)
         low = (own_fade - high.astype(F32)).astype(BF16)
-        packed = jnp.concatenate([own.astype(BF16), high, low], axis=0)
+        packed = jnp.concatenate([own.astype(BF16), high, low], axis=1)
         got = passed_along(packed, "tm", distance).astype(F32)
         reached = here >= distance
-        got_fade = jnp.where(reached, got[size : size + 1] + got[size + 1 : size + 2], 1.0)
-        total = total + fade * got[:size]
+        got_fade = jnp.where(reached, got[:, size : size + 1] + got[:, size + 1 : size + 2], 1.0)
+        total = total + fade * got[:, :size]
         fade = fade * got_fade
         distance *= 2
     return total
@@ -230,7 +335,6 @@
     devices = lax.axis_size("tm") * lax.axis_size("table")
     capacity = max(2 * events // devices, 2)
     blocks = events // BLOCK
-    slots_all = devices * capacity
 
     owners = item_owner[..., 0]
     owner_match = owners[..., None] == jnp.arange(devices, dtype=jnp.int32)
@@ -252,136 +356,151 @@
     ).astype(BF16)
     asked = jnp.einsum("utd,utc->duc", owner_hot, parts, preferred_element_type=F32)
     requests = (64.0 * asked[..., :capacity] + asked[..., capacity:]).astype(jnp.int32)
-    wanted = lax.all_to_all(requests, ("tm", "table"), split_axis=0, concat_axis=0, tiled=True)
-    place = owners * capacity + slots
+    slot_rows = -(-capacity // 16) * 16
+    slots_all = devices * slot_rows
+    requests = jnp.pad(requests, ((0, 0), (0, 0), (0, slot_rows - capacity)))
+    requests = requests.reshape(devices, 1, user_count * slot_rows)
+    lanes = -(-user_count * slot_rows // 128) * 128
+    requests = jnp.pad(requests, ((0, 0), (0, 0), (0, lanes - user_count * slot_rows)))
+    here = lax.axis_index("tm") * lax.axis_size("table") + lax.axis_index("table")
+    place = ((owners - here) % devices) * slot_rows + slots
+    group = 4
+    buffer = (user_count, devices, slot_rows, model_dim)
+    fetched = pl.pallas_call(
+        lambda *refs: exchange_kernel(devices, group, *refs),
+        in_specs=[pl.BlockSpec(memory_space=pltpu.VMEM), pl.BlockSpec(memory_space=pl.ANY)],
+        out_specs=pl.BlockSpec(memory_space=pl.ANY),
+        out_shape=struct(buffer, BF16),
+        scratch_shapes=[
+            pltpu.VMEM(item_table.shape, BF16),
+            pltpu.VMEM((8, lanes), F32),
+            pltpu.VMEM((devices, 1, lanes), jnp.int32),
+            pltpu.VMEM(buffer, BF16),
+            pltpu.SemaphoreType.DMA,
+            pltpu.SemaphoreType.DMA,
+            pltpu.SemaphoreType.DMA((devices,)),
+            pltpu.SemaphoreType.DMA((devices,)),
+            pltpu.SemaphoreType.DMA((devices,)),
+            pltpu.SemaphoreType.DMA((devices,)),
+        ],
+        compiler_params=pltpu.CompilerParams(
+            vmem_limit_bytes=VMEM_LIMIT, collective_id=0, has_side_effects=True
+        ),
+        cost_estimate=cost(13 << 30, 10 << 20),
+        name="exchange",
+    )(requests, item_table).reshape(user_count, slots_all, model_dim)
 
     positions = lax.axis_index("tm") * events + jnp.arange(events, dtype=jnp.int32)
     alive = (positions[None, :] < history_len[:, None]).astype(F32)
 
-    fetched = []
-    for user in range(user_count):
-        sent = jnp.take(item_table, wanted[:, user].reshape(-1), axis=0, mode="clip")
-        fetched.append(
-            lax.all_to_all(
-                sent.reshape(devices, capacity, model_dim),
-                ("tm", "table"),
-                split_axis=0,
-                concat_axis=0,
-                tiled=True,
-            ).reshape(slots_all, model_dim)
-        )
-
-    outputs = []
-    for user in range(user_count):
-        alive_column = alive[user][:, None]
-        item, gate, conv, step = pl.pallas_call(
-            lambda *refs: project_kernel(inner_dim, conv_dim, *refs),
-            grid=(blocks,),
+    alive_column = alive[..., None]
+    item, gate, conv, step = pl.pallas_call(
+        lambda *refs: project_kernel(inner_dim, conv_dim, *refs),
+        grid=(user_count, blocks),
+        in_specs=[
+            rows_of(1),
+            user_of(slots_all, model_dim),
+            whole(1, model_dim),
+            whole(model_dim, projected_dim),
+        ],
+        out_specs=[rows_of(model_dim), rows_of(inner_dim), rows_of(conv_dim), rows_of(head_count)],
+        out_shape=[
+            struct((user_count, events, model_dim), BF16),
+            struct((user_count, events, inner_dim), BF16),
+            struct((user_count, events, conv_dim), BF16),
+            struct((user_count, events, head_count), F32),
+        ],
+        compiler_params=params(),
+        cost_estimate=cost(2 * events * model_dim * (projected_dim + slots_all), 9 << 20),
+        name="project",
+    )(place[..., None], fetched, norm_gain[None], in_weight)
+    edge = passed_along(conv[:, events - 8 :], "tm", 1)
+    x, bc, steps, cum, entering, before, final, factor = pl.pallas_call(
+        lambda *refs: state_kernel(inner_dim, *refs),
+        grid=(user_count, blocks),
+        in_specs=[
+            rows_of(conv_dim),
+            rows_of(head_count),
+            rows_of(1),
+            rows_of(1),
+            user_of(8, conv_dim),
+            whole(4, conv_dim),
+            whole(1, conv_dim),
+            whole(1, head_count),
+            whole(1, head_count),
+        ],
+        out_specs=[
+            rows_of(inner_dim),
+            rows_of(2 * state_dim),
+            rows_of(head_count),
+            rows_of(head_count),
+            one_of(state_dim, inner_dim),
+            one_of(8, inner_dim),
+            user_of(state_dim, inner_dim),
+            user_of(8, inner_dim),
+        ],
+        out_shape=[
+            struct((user_count, events, inner_dim), BF16),
+            struct((user_count, events, 2 * state_dim), BF16),
+            struct((user_count, events, head_count), F32),
+            struct((user_count, events, head_count), F32),
+            struct((user_count, blocks, state_dim, inner_dim), F32),
+            struct((user_count, blocks, 8, inner_dim), F32),
+            struct((user_count, state_dim, inner_dim), F32),
+            struct((user_count, 8, inner_dim), F32),
+        ],
+        scratch_shapes=[
+            pltpu.VMEM((BLOCK + 8, conv_dim), F32),
+            pltpu.VMEM((state_dim, inner_dim), F32),
+            pltpu.VMEM((8, head_count), F32),
+        ],
+        compiler_params=params(),
+        cost_estimate=cost(4 << 30, 8 << 20, events * conv_dim),
+        name="states",
+    )(
+        conv, step, event_gap[..., None], alive_column, edge,
+        conv_weight, conv_bias[None], dt_bias[None], decay_rate[None],
+    )
+    incoming = earlier_spans(final, factor[:, 0:1])
+    y = pl.pallas_call(
+        local_kernel,
+        grid=(user_count, blocks),
+        in_specs=[
+            rows_of(inner_dim), rows_of(2 * state_dim), rows_of(head_count), rows_of(head_count),
+        ],
+        out_specs=rows_of(inner_dim),
+        out_shape=struct((user_count, events, inner_dim), F32),
+        compiler_params=params(),
+        cost_estimate=cost(8 << 30, 5 << 20, events * BLOCK * head_count),
+        name="local",
+    )(x, bc, steps, cum)
+    return (
+        pl.pallas_call(
+            emit_kernel,
+            grid=(user_count, blocks),
             in_specs=[
-                rows_of(1),
-                whole(slots_all, model_dim),
-                whole(1, model_dim),
-                whole(model_dim, projected_dim),
-            ],
-            out_specs=[rows_of(model_dim), rows_of(inner_dim), rows_of(conv_dim), rows_of(head_count)],
-            out_shape=[
-                struct((events, model_dim), BF16),
-                struct((events, inner_dim), BF16),
-                struct((events, conv_dim), BF16),
-                struct((events, head_count), F32),
-            ],
-            compiler_params=params(),
-            cost_estimate=cost(2 * events * model_dim * (projected_dim + slots_all), 9 << 20),
-            name="project",
-        )(place[user][:, None], fetched[user], norm_gain[None], in_weight)
-        edge = passed_along(conv[events - 8 :], "tm", 1)
-        x, bc, steps, cum, entering, before, final, factor = pl.pallas_call(
-            lambda *refs: state_kernel(inner_dim, *refs),
-            grid=(blocks,),
-            in_specs=[
-                rows_of(conv_dim),
-                rows_of(head_count),
-                rows_of(1),
-                rows_of(1),
-                whole(8, conv_dim),
-                whole(4, conv_dim),
-                whole(1, conv_dim),
-                whole(1, head_count),
-                whole(1, head_count),
-            ],
-            out_specs=[
                 rows_of(inner_dim),
                 rows_of(2 * state_dim),
                 rows_of(head_count),
-                rows_of(head_count),
+                rows_of(inner_dim),
+                rows_of(model_dim),
+                rows_of(1),
                 one_of(state_dim, inner_dim),
                 one_of(8, inner_dim),
-                whole(state_dim, inner_dim),
-                whole(8, inner_dim),
+                user_of(state_dim, inner_dim),
+                whole(1, inner_dim),
+                whole(inner_dim, model_dim),
             ],
-            out_shape=[
-                struct((events, inner_dim), BF16),
-                struct((events, 2 * state_dim), BF16),
-                struct((events, head_count), F32),
-                struct((events, head_count), F32),
-                struct((blocks, state_dim, inner_dim), F32),
-                struct((blocks, 8, inner_dim), F32),
-                struct((state_dim, inner_dim), F32),
-                struct((8, inner_dim), F32),
-            ],
-            scratch_shapes=[
-                pltpu.VMEM((BLOCK + 8, conv_dim), F32),
-                pltpu.VMEM((state_dim, inner_dim), F32),
-                pltpu.VMEM((8, head_count), F32),
-            ],
+            out_specs=rows_of(model_dim),
+            out_shape=struct((user_count, events, model_dim), BF16),
             compiler_params=params(),
-            cost_estimate=cost(4 << 30, 8 << 20, events * conv_dim),
-            name="states",
+            cost_estimate=cost(4 << 30, 9 << 20, events * inner_dim),
+            name="emit",
         )(
-            conv, step, event_gap[user][:, None], alive_column, edge,
-            conv_weight, conv_bias[None], dt_bias[None], decay_rate[None],
+            y, bc, cum, gate, item, alive_column, entering, before, incoming,
+            out_gain[None], emitted_projection,
         )
-        incoming = earlier_spans(final, factor[0:1])
-        y = pl.pallas_call(
-            local_kernel,
-            grid=(blocks,),
-            in_specs=[
-                rows_of(inner_dim), rows_of(2 * state_dim), rows_of(head_count), rows_of(head_count),
-            ],
-            out_specs=rows_of(inner_dim),
-            out_shape=struct((events, inner_dim), F32),
-            compiler_params=params(),
-            cost_estimate=cost(8 << 30, 5 << 20, events * BLOCK * head_count),
-            name="local",
-        )(x, bc, steps, cum)
-        outputs.append(
-            pl.pallas_call(
-                emit_kernel,
-                grid=(blocks,),
-                in_specs=[
-                    rows_of(inner_dim),
-                    rows_of(2 * state_dim),
-                    rows_of(head_count),
-                    rows_of(inner_dim),
-                    rows_of(model_dim),
-                    rows_of(1),
-                    one_of(state_dim, inner_dim),
-                    one_of(8, inner_dim),
-                    whole(state_dim, inner_dim),
-                    whole(1, inner_dim),
-                    whole(inner_dim, model_dim),
-                ],
-                out_specs=rows_of(model_dim),
-                out_shape=struct((events, model_dim), BF16),
-                compiler_params=params(),
-                cost_estimate=cost(4 << 30, 9 << 20, events * inner_dim),
-                name="emit",
-            )(
-                y, bc, cum, gate, item, alive_column, entering, before, incoming,
-                out_gain[None], emitted_projection,
-            )
-        )
-    return jnp.stack(outputs)
+    )
 
 
 def solution(mesh):

time: 182 us -> 203 us (1.12); the launches traced: 181 us -> 199 us
  Pallas kernels: 46.7 us -> 129 us
  waiting for transfers between devices: 59.5 us -> 25.6 us
  starting transfers between devices: 29.4 us -> 6.39 us
  blocking collectives: 8.92 us -> 0 us
  other arithmetic: 2.93 us -> 7.2 us
  local copies, waits for them, and re-layouts: 32.9 us -> 29.7 us
    pallas_call x6 -> x4, Pallas kernels: 36.1 us -> 120 us  [the longest x1 82.1 us: per_device(): pl.pallas_call(lambda *refs: exchange_kernel(devices, group, *refs), in_s...]
    all_to_all x2 -> x0, waiting for transfers between devices: 41 us -> none  [per_device(): lax.all_to_all(sent.reshape(devices, capacity, model_dim), ('tm', 'table'...]
    gather x2 -> x0, local copies, waits for them, and re-layouts: 16.4 us -> none  [per_device(): jnp.take(item_table, wanted[:, user].reshape(-1), axis=0, mode='clip')]
    all_to_all x2 -> x0, starting transfers between devices: 12.9 us -> none  [per_device(): lax.all_to_all(sent.reshape(devices, capacity, model_dim), ('tm', 'table'...]
    unnamed x48 -> x67, local copies, waits for them, and re-layouts: 12.1 us -> 24.8 us
    ppermute x8 -> x4, starting transfers between devices: 16.5 us -> 6.39 us  [passed_along(): return lax.ppermute(block, axis, route)]
    all_to_all x1 -> x0, blocking collectives: 8.92 us -> none  [per_device(): lax.all_to_all(requests, ('tm', 'table'), split_axis=0, concat_axis=0, ti...]
    ppermute x8 -> x4, waiting for transfers between devices: 18.5 us -> 25.6 us  [passed_along(): return lax.ppermute(block, axis, route)]
  transfers between devices with their start and end apart: 10 -> 4, of which waited for: 5 -> 4; matrix products, arithmetic and copies ran while one was open for 9% -> 1% of each run, Pallas kernels for 18% -> 4%
where the time goes in v2:
time: 203 us; the launch traced here: 199 us
  Pallas kernels  129 us (64%)
  local copies, waits for them, and re-layouts  29.7 us (15%)
  waiting for transfers between devices  25.6 us (13%)
  other arithmetic  7.2 us (4%)
  starting transfers between devices  6.39 us (3%)
    pallas_call x1, Pallas kernels, per_device(): pl.pallas_call(lambda *refs: exchange_kernel(devices, group, *refs), in_s...  82.1 us
    ppermute x4, waiting for transfers between devices, passed_along(): return lax.ppermute(block, axis, route)  25.6 us
    unnamed x67, local copies, waits for them, and re-layouts  24.8 us
    pallas_call x1, Pallas kernels, per_device(): pl.pallas_call(lambda *refs: state_kernel(inner_dim, *refs), grid=(user_c...  15.2 us
    pallas_call x1, Pallas kernels, per_device(): pl.pallas_call(emit_kernel, grid=(user_count, blocks), in_specs=[rows_of(...  13.8 us
    pallas_call x1, Pallas kernels, per_device(): pl.pallas_call(lambda *refs: project_kernel(inner_dim, conv_dim, *refs),...  9.82 us
    pallas_call x1, Pallas kernels, per_device(): pl.pallas_call(local_kernel, grid=(user_count, blocks), in_specs=[rows_of...  8.39 us
    ppermute x4, starting transfers between devices, passed_along(): return lax.ppermute(block, axis, route)  6.39 us
  transfers between devices with their start and end apart: 4, of which 4 were waited for; matrix products, arithmetic and copies ran while one was open for 1% of the time, Pallas kernels for 4%

profile of v2, /device:TPU:26, one launch (start us, length us, event | category | flops | bytes accessed | tf_op | source)
XLA Modules:
  0.0 199.3 jit_solution(7543719956501106754)
XLA Ops:
  0.0 0.7 copy.57
  0.7 0.4 fusion.9
  1.1 0.7 broadcast_compare_fusion
  1.8 0.7 multiply_subtract_fusion
  2.5 0.4 copy.37
  3.0 0.2 convolution_bitcast_fusion
  3.2 0.1 fusion.21
  3.3 0.1 reshape.68
  3.4 1.2 copy.34
  4.6 1.2 copy.39
  5.8 2.8 %copy.41.refs_3_ = bf16[512,2192]{1,0:T(8,128)(2,1)S(1)} copy(bf16[512,2192]{0,1:T(8,128)(2,1)} %param.19) | data formatting | bytes 4489216 | tf_op args[6]
  8.6 0.0 copy-start.11
  8.6 2.2 %copy-done.11 = bf16[4096,512]{1,0:T(8,128)(2,1)S(1)} copy-done((bf16[4096,512]{1,0:T(8,128)(2,1)S(1)}, bf16[4096,512]{1,0:T(8,128)(2,1)}, u32[]{:S(2)}) %copy-start.11) | copy-done | bytes 4194328
  10.8 82.1 %exchange.1 = bf16[2,32,48,512]{3,2,1,0:T(8,128)(2,1)S(1)} custom-call(s32[32,1,128]{2,1,0:T(1,128)S(1)} %pad.4.refs_0_, bf16[4096,512]{1,0:T(8,128)(2,1)S(1)} %copy-done.11), custom_call_target="tpu_custom_call" | custom-call | flops 13958643712 | bytes 10485760 | tf_op jit(solution)/shard_map/exchange/pallas_call | solution.py:369
  92.9 0.0 copy-done.26
  92.9 0.0 copy-done.27
  92.9 0.0 copy-start.15
  92.9 0.4 fusion.14.refs_0_
  93.3 0.3 copy-done.15
  93.6 0.0 copy-start.17
  93.6 9.8 %project.1 = (bf16[2,768,512]{2,1,0:T(8,128)(2,1)S(1)}, bf16[2,768,1024]{2,1,0:T(8,128)(2,1)S(1)}, bf16[2,768,1152]{2,1,0:T(8,128)(2,1)}, f32[2,768,16]{2,1,0:T(8,128)S(1)}) custom-call(s32[2,768,1]{2,1,0:T(8,128)S(1)} %fusion.14.refs_0_, bf16[2,1536,512]{2,1,0:T(8,128)(2,1)S(1)} %bitcast.43, f32[1,512]{1,0:T(1,128)S(1)} %bitcast.40, ...), custom_call_target="tpu_custom_call" | custom-call | flops 2931818496 | bytes 9437184 | tf_op jit(solution)/shard_map/project/pallas_call | solution.py:397
  103.4 1.7 copy-done.1
  105.1 1.1 copy-done.3
  106.3 0.9 copy-done.18
  107.2 0.8 slice.38
  107.9 1.9 collective-permute-start
  109.9 0.0 copy-done.30
  109.9 0.2 compare_convert_fusion.refs_3_.alive
  110.0 0.0 copy-done.28
  110.1 0.0 copy-done.29
  110.1 1.2 copy.42.refs_2_
  111.3 3.4 %collective-permute-done.refs_4_ = bf16[2,8,1152]{2,1,0:T(8,128)(2,1)S(1)} collective-permute-done((bf16[2,8,1152]{2,1,0:T(8,128)(2,1)S(1)}, bf16[2,8,1152]{2,1,0:T(8,128)(2,1)S(1)}, u32[]{:S(2)}, u32[]{:S(2)}) %collective-permute-start) | collective-permute-done | bytes 36896 | tf_op jit(solution)/shard_map/ppermute | solution.py:17
  114.7 0.6 copy-done.12
  115.3 0.0 copy-done.16
  115.3 0.0 copy-done.17
  115.3 1.1 copy-done.8
  116.4 2.0 %copy-done.10 = bf16[2,768,1152]{2,1,0:T(8,128)(2,1)S(1)} copy-done((bf16[2,768,1152]{2,1,0:T(8,128)(2,1)S(1)}, bf16[2,768,1152]{2,1,0:T(8,128)(2,1)}, u32[]{:S(2)}) %copy-start.10) | copy-done | bytes 3538968
  118.4 0.8 copy-done.13
  119.2 0.7 copy-done.14
  119.9 1.1 copy-done.19
  121.0 15.2 %states.1 = (bf16[2,768,1024]{2,1,0:T(8,128)(2,1)S(1)}, bf16[2,768,128]{2,1,0:T(8,128)(2,1)S(1)}, f32[2,768,16]{2,1,0:T(8,128)S(1)}, f32[2,768,16]{2,1,0:T(8,128...) custom-call(bf16[2,768,1152]{2,1,0:T(8,128)(2,1)S(1)} %copy-done.10,, ...), custom_call_target="tpu_custom_call" | custom-call | flops 4294967296 | bytes 8388608 | tf_op jit(solution)/shard_map/states/pallas_call | solution.py:418
  136.3 0.0 copy-start.6
  136.3 0.9 copy-done.6
  137.2 1.6 copy-done.20
  138.8 0.9 copy-done.22
  139.8 0.8 pad_maximum_fusion
  140.5 1.9 collective-permute-start.1
  142.5 10.8 %collective-permute-done.1 = bf16[2,66,1024]{2,1,0:T(8,128)(2,1)} collective-permute-done((bf16[2,66,1024]{2,1,0:T(8,128)(2,1)}, bf16[2,66,1024]{2,1,0:T(8,128)(2,1)}, u32[]{:S(2)}, u32[]{:S(2)}) %collective-permute-start.1) | collective-permute-done | bytes 270368 | tf_op jit(solution)/shard_map/ppermute | solution.py:17
  153.3 1.0 convert_element_type.82
  154.3 0.8 copy-done.24
  155.1 0.1 add_convert_fusion.1
  155.2 0.8 pad_maximum_fusion.1
  156.0 1.3 collective-permute-start.2
  157.3 9.7 %collective-permute-done.2 = bf16[2,66,1024]{2,1,0:T(8,128)(2,1)} collective-permute-done((bf16[2,66,1024]{2,1,0:T(8,128)(2,1)}, bf16[2,66,1024]{2,1,0:T(8,128)(2,1)}, u32[]{:S(2)}, u32[]{:S(2)}) %collective-permute-start.2) | collective-permute-done | bytes 270368 | tf_op jit(solution)/shard_map/ppermute | solution.py:17
  166.9 1.0 convert_element_type.87
  168.0 1.2 add_convert_fusion
  169.2 1.3 collective-permute-start.3
  170.6 1.9 copy-done.21
  172.5 8.4 %local.1.y = f32[2,768,1024]{2,1,0:T(8,128)S(1)} custom-call(bf16[2,768,1024]{2,1,0:T(8,128)(2,1)S(1)} %copy-done.21, bf16[2,768,128]{2,1,0:T(8,128)(2,1)S(1)} %get-tuple-element.20.bc, f32[2,768,16]{2,1,0:T(8,128)S(1)} %copy-done.23, f32[2,768,16]{2,1,0:T(8,128)S(1)} %copy-done.7), custom_call_target="tpu_custom_call" | custom-call | flops 8589934592 | bytes 5242880 | tf_op jit(solution)/shard_map/local/pallas_call | solution.py:465
  180.9 2.6 %copy-done = f32[2,768,1024]{2,1,0:T(8,128)} copy-done((f32[2,768,1024]{2,1,0:T(8,128)}, f32[2,768,1024]{2,1,0:T(8,128)S(1)}, u32[]{:S(2)}) %copy-start) | copy-done | bytes 6291480
  183.5 1.8 collective-permute-done.3
  185.3 0.0 copy-done.25
  185.3 0.1 multiply_add_fusion.incoming
  185.4 13.8 %emit.1 = bf16[2,768,512]{2,1,0:T(8,128)(2,1)} custom-call(f32[2,768,1024]{2,1,0:T(8,128)} %copy-done, bf16[2,768,128]{2,1,0:T(8,128)(2,1)S(1)} %get-tuple-element.20.bc, f32[2,768,16]{2,1,0:T(8,128)S(1)} %copy-done.7, bf16[2,768,1024]{2,1,0:T(8,128)(2,1)S(1)} %copy-done.2, bf16[2,768,512]{2,1,0:T(8,128)(2,1)S(1)} %copy-done.4, ...), custom_call_target="tpu_custom_call" | custom-call | flops 4294967296 | bytes 9437184 | tf_op jit(solution)/shard_map/emit/pallas_call | solution.py:478
  (51 shorter events, 0.4 us)
Async XLA Ops:
  8.6 2.2 %copy-start.11 = (bf16[4096,512]{1,0:T(8,128)(2,1)S(1)}, bf16[4096,512]{1,0:T(8,128)(2,1)}, u32[]{:S(2)}) copy-start(bf16[4096,512]{1,0:T(8,128)(2,1)} %refs_1_.1) | copy-start | bytes 12582916
  10.8 82.1 %copy-start.26 = (s32[2,768,1]{2,1,0:T(8,128)S(1)}, s32[2,768,1]{2,1,0:T(8,128)}, u32[]{:S(2)}) copy-start(s32[2,768,1]{2,1,0:T(8,128)} %copy.34) | copy-start | bytes 18436
  10.8 82.1 %copy-start.27 = (s32[2,768,1]{2,1,0:T(8,128)S(1)}, s32[2,768,1]{2,1,0:T(8,128)}, u32[]{:S(2)}) copy-start(s32[2,768,1]{2,1,0:T(8,128)} %copy.39) | copy-start | bytes 18436
  92.9 0.7 copy-start.15
  93.6 16.3 %copy-start.30 = (s32[2]{0:T(128)S(1)}, s32[2]{0:T(128)}, u32[]{:S(2)}) copy-start(s32[2]{0:T(128)} %param.15) | copy-start | bytes 28
  93.6 16.5 %copy-start.28 = (f32[1152]{0:T(1024)S(1)}, f32[1152]{0:T(1024)}, u32[]{:S(2)}) copy-start(f32[1152]{0:T(1024)} %param.21) | copy-start | bytes 13828
  93.6 16.5 %copy-start.29 = (f32[2,768]{1,0:T(2,128)S(1)}, f32[2,768]{1,0:T(2,128)}, u32[]{:S(2)}) copy-start(f32[2,768]{1,0:T(2,128)} %param.16) | copy-start | bytes 18436
  93.6 21.7 %copy-start.16 = (f32[16]{0:T(128)S(1)}, f32[16]{0:T(128)}, u32[]{:S(2)}) copy-start(f32[16]{0:T(128)} %param.22) | copy-start | bytes 196
  93.6 21.7 %copy-start.17 = (f32[16]{0:T(128)S(1)}, f32[16]{0:T(128)}, u32[]{:S(2)}) copy-start(f32[16]{0:T(128)} %param.23) | copy-start | bytes 196
  103.4 1.7 copy-start.1
  105.1 1.1 copy-start.3
  106.3 0.9 copy-start.18
  107.9 6.7 %collective-permute-start = (bf16[2,8,1152]{2,1,0:T(8,128)(2,1)S(1)}, bf16[2,8,1152]{2,1,0:T(8,128)(2,1)S(1)}, u32[]{:S(2)}, u32[]{:S(2)}) collective-permute-start(bf16[2,8,1152]{2,1,0:T(8,128)(2,1)S(1)} %slice.38), channel_id=1, source_target_pairs={{0,4},{4,8},{8,12},{12,16},{16,20},{20,24},{24,28},{1,5},{5,9},{9,... | collective-permute-start | bytes 110600 | tf_op jit(solution)/shard_map/ppermute | solution.py:17
  114.7 0.6 copy-start.12
  115.3 1.1 copy-start.8
  116.4 2.0 %copy-start.10 = (bf16[2,768,1152]{2,1,0:T(8,128)(2,1)S(1)}, bf16[2,768,1152]{2,1,0:T(8,128)(2,1)}, u32[]{:S(2)}) copy-start(bf16[2,768,1152]{2,1,0:T(8,128)(2,1)} %get-tuple-element.17.refs_0_) | copy-start | bytes 10616836
  118.4 0.8 copy-start.13
  119.2 0.7 copy-start.14
  119.9 1.1 copy-start.19
  136.3 0.9 copy-start.6
  137.2 1.6 copy-start.20
  138.8 0.9 copy-start.22
  140.5 12.7 %collective-permute-start.1 = (bf16[2,66,1024]{2,1,0:T(8,128)(2,1)}, bf16[2,66,1024]{2,1,0:T(8,128)(2,1)}, u32[]{:S(2)}, u32[]{:S(2)}) collective-permute-start(bf16[2,66,1024]{2,1,0:T(8,128)(2,1)} %pad_maximum_fusion), channel_id=1, source_target_pairs={{0,4},{4,8},{8,12},{12,16},{16,20},{20,24},{24,28},{1,5},{5,9},{9,... | collective-permute-start | bytes 811016 | tf_op jit(solution)/shard_map/ppermute | solution.py:17
  154.3 0.8 copy-start.24
  156.0 11.0 %collective-permute-start.2 = (bf16[2,66,1024]{2,1,0:T(8,128)(2,1)}, bf16[2,66,1024]{2,1,0:T(8,128)(2,1)}, u32[]{:S(2)}, u32[]{:S(2)}) collective-permute-start(bf16[2,66,1024]{2,1,0:T(8,128)(2,1)} %pad_maximum_fusion.1), channel_id=1, source_target_pairs={{0,8},{4,12},{8,16},{12,20},{16,24},{20,28},{1,9},{5,13},{9,17},{1... | collective-permute-start | bytes 811016 | tf_op jit(solution)/shard_map/ppermute | solution.py:17
  157.2 13.3 %copy-start.7 = (f32[2,768,16]{2,1,0:T(8,128)S(1)}, f32[2,768,16]{2,1,0:T(8,128)}, u32[]{:S(2)}) copy-start(f32[2,768,16]{2,1,0:T(8,128)} %copy-done.6) | copy-start | bytes 294916
  157.3 13.3 %copy-start.23 = (f32[2,768,16]{2,1,0:T(8,128)S(1)}, f32[2,768,16]{2,1,0:T(8,128)}, u32[]{:S(2)}) copy-start(f32[2,768,16]{2,1,0:T(8,128)} %copy-done.22) | copy-start | bytes 294916
  169.2 16.0 %collective-permute-start.3 = (bf16[2,66,1024]{2,1,0:T(8,128)(2,1)S(1)}, bf16[2,66,1024]{2,1,0:T(8,128)(2,1)S(1)}, u32[]{:S(2)}, u32[]{:S(2)}) collective-permute-start(bf16[2,66,1024]{2,1,0:T(8,128)(2,1)S(1)} %pad_maximum_fusion.2), channel_id=1, source_target_pairs={{0,16},{4,20},{8,24},{12,28},{1,17},{5,21},{9,25},{13,29},{2,18},{... | collective-permute-start | bytes 811016 | tf_op jit(solution)/shard_map/ppermute | solution.py:17
  170.6 1.9 copy-start.21
  172.4 12.8 %copy-start.25 = (f32[2,66,1024]{2,1,0:T(8,128)S(1)}, f32[2,66,1024]{2,1,0:T(8,128)}, u32[]{:S(2)}) copy-start(f32[2,66,1024]{2,1,0:T(8,128)} %copy-done.24) | copy-start | bytes 1622020
  172.4 12.9 %copy-start.2 = (bf16[2,768,1024]{2,1,0:T(8,128)(2,1)S(1)}, bf16[2,768,1024]{2,1,0:T(8,128)(2,1)}, u32[]{:S(2)}) copy-start(bf16[2,768,1024]{2,1,0:T(8,128)(2,1)} %copy-done.1) | copy-start | bytes 9437188
  172.4 12.9 %copy-start.5 = (bf16[1024,512]{1,0:T(8,128)(2,1)S(1)}, bf16[1024,512]{1,0:T(8,128)(2,1)}, u32[]{:S(2)}) copy-start(bf16[1024,512]{1,0:T(8,128)(2,1)} %weight.1) | copy-start | bytes 3145732
  172.5 13.0 %copy-start.9 = (f32[1024]{0:T(1024)S(1)}, f32[1024]{0:T(1024)}, u32[]{:S(2)}) copy-start(f32[1024]{0:T(1024)} %param.24) | copy-start | bytes 12292
  180.8 2.6 %copy-start = (f32[2,768,1024]{2,1,0:T(8,128)}, f32[2,768,1024]{2,1,0:T(8,128)S(1)}, u32[]{:S(2)}) copy-start(f32[2,768,1024]{2,1,0:T(8,128)S(1)} %local.1.y) | copy-start | bytes 18874372
  183.5 1.9 copy-start.4

commit v3 on v2

--- a/solution.py
+++ b/solution.py
@@ -159,7 +159,7 @@
 
 def state_kernel(
     inner_dim, conv, step, gap, alive, edge, taps, bias, dt_bias, rate,
-    x_out, bc_out, steps_out, cum_out, entering, before, final, factor,
+    x_out, bc_out, cum_out, entering, before, final, factor,
     padded, running, gone,
 ):
     head_count = step.shape[1]
@@ -180,7 +180,6 @@
     out = silu(total).astype(BF16)
     x = out[:, :inner_dim]
     bc = out[:, inner_dim:]
-    x_out[...] = x
     bc_out[...] = bc
     raw = step[...] + dt_bias[...]
     soft = jnp.maximum(raw, 0.0) + jnp.log1p(jnp.exp(-jnp.abs(raw)))
@@ -193,10 +192,10 @@
         jnp.where(below, 1.0, 0.0), log_decay, preferred_element_type=F32,
         precision=lax.Precision.HIGHEST,
     )
-    steps_out[...] = steps
     cum_out[...] = cum
     last = cum[BLOCK - 1 : BLOCK]
     spread = head_spread(head_count, inner_dim)
+    x_out[...] = (over_channels(steps, spread) * x.astype(F32)).astype(BF16)
     scaled = (over_channels(jnp.exp(last - cum) * steps, spread) * x.astype(F32)).astype(BF16)
     block_state = lax.dot_general(
         bc[:, :state_dim], scaled, (((0,), (0,)), ((), ())), preferred_element_type=F32
@@ -211,32 +210,120 @@
     factor[...] = over_channels(jnp.exp(gone[...]), spread)
 
 
-def local_kernel(x, bc, steps, cum, y):
-    head_count = steps.shape[1]
-    inner_dim = x.shape[1]
-    state_dim = bc.shape[1] // 2
-    spread = head_spread(head_count, inner_dim)
-    xs = (over_channels(steps[...], spread) * x[...].astype(F32)).astype(BF16)
-    scores = lax.dot_general(
-        bc[:, state_dim:], bc[:, :state_dim], (((1,), (1,)), ((), ())),
-        preferred_element_type=F32,
-    )
+def local_kernel(
+    head_count, xs, bc, cum, state, factor,
+    y, incoming, scores, across, inbox, outbox, send_sem, recv_sem,
+):
+    length, here = (lax.axis_size("tm"), lax.axis_index("tm"))
+    users, events, inner_dim = xs.shape
+    state_dim = bc.shape[2] // 2
+    blocks = events // BLOCK
+    width = 2 * (inner_dim // head_count)
+    pairs = head_count // 2
+    chunks = users * pairs
+    delay = 2
+
+    barrier = pltpu.get_barrier_semaphore()
+
+    @pl.when(here > 0)
+    def _():
+        pl.semaphore_signal(
+            barrier, inc=1, device_id=(jnp.maximum(here - 1, 0), lax.axis_index("table")),
+            device_id_type=pl.DeviceIdType.MESH,
+        )
+
+    @pl.when(here < length - 1)
+    def _():
+        pl.semaphore_signal(
+            barrier, inc=1,
+            device_id=(jnp.minimum(here + 1, length - 1), lax.axis_index("table")),
+            device_id_type=pl.DeviceIdType.MESH,
+        )
+
+    pl.semaphore_wait(barrier, jnp.minimum(here, 1) + jnp.minimum(length - 1 - here, 1))
+
+    def onward(c):
+        return pltpu.make_async_remote_copy(
+            src_ref=outbox.at[c],
+            dst_ref=inbox.at[c],
+            send_sem=send_sem.at[c],
+            recv_sem=recv_sem.at[c],
+            device_id=(jnp.minimum(here + 1, length - 1), lax.axis_index("table")),
+            device_id_type=pl.DeviceIdType.MESH,
+        )
+
+    def pass_chunk(c):
+        user = c % users
+        lanes = pl.ds(pl.multiple_of((c // users) * width, width), width)
+
+        @pl.when(here == 0)
+        def _():
+            incoming[user, :, lanes] = jnp.zeros((state_dim, width), F32)
+
+        @pl.when(here > 0)
+        def _():
+            onward(c).wait_recv()
+            incoming[user, :, lanes] = inbox[c].astype(F32)
+
+        @pl.when(here < length - 1)
+        def _():
+            after = factor[user, 0:1, lanes] * incoming[user, :, lanes] + state[user, :, lanes]
+            outbox[c] = after.astype(BF16)
+            onward(c).start()
+
+    def slot(t):
+        c = t - delay * here
+
+        @pl.when((c >= 0) & (c < chunks))
+        def _():
+            pass_chunk(c)
+
     below = lax.broadcasted_iota(jnp.int32, (BLOCK, BLOCK), 0) >= lax.broadcasted_iota(
         jnp.int32, (BLOCK, BLOCK), 1
     )
-    scores = jnp.where(below, scores, 0.0)
-    down = cum[...]
-    across = down.T
-    width = 2 * (inner_dim // head_count)
+
+    @pl.loop(0, users * blocks)
+    def _(r):
+        rows = pl.ds(pl.multiple_of((r % blocks) * BLOCK, BLOCK), BLOCK)
+        both = bc[r // blocks, rows, :]
+        found = lax.dot_general(
+            both[:, state_dim:], both[:, :state_dim], (((1,), (1,)), ((), ())),
+            preferred_element_type=F32,
+        )
+        scores[r] = jnp.where(below, found, 0.0)
+        across[r] = cum[r // blocks, rows, :].T
+
     left = lax.broadcasted_iota(jnp.int32, (BLOCK, width), 1) < width // 2
-    for pair in range(head_count // 2):
+    for pair in range(pairs):
         lanes = slice(pair * width, (pair + 1) * width)
-        parts = []
-        for h in (2 * pair, 2 * pair + 1):
-            fading = jnp.exp(jnp.minimum(down[:, h : h + 1] - across[h : h + 1], 0.0))
-            mixing = (scores * fading).astype(BF16)
-            parts.append(jnp.dot(mixing, xs[:, lanes], preferred_element_type=F32))
-        y[:, lanes] = jnp.where(left, parts[0], parts[1])
+
+        @pl.loop(0, users * blocks)
+        def _(r, pair=pair, lanes=lanes):
+            user = r // blocks
+
+            @pl.when(r % blocks == 0)
+            def _():
+                slot(pair * users + user)
+
+            rows = pl.ds(pl.multiple_of((r % blocks) * BLOCK, BLOCK), BLOCK)
+            values = xs[user, rows, lanes]
+            parts = []
+            for h in (2 * pair, 2 * pair + 1):
+                down = cum[user, rows, h : h + 1]
+                fading = jnp.exp(jnp.minimum(down - across[r, h : h + 1, :], 0.0))
+                mixing = (scores[r] * fading).astype(BF16)
+                parts.append(jnp.dot(mixing, values, preferred_element_type=F32))
+            y[user, rows, lanes] = jnp.where(left, parts[0], parts[1]).astype(BF16)
+
+    @pl.loop(chunks, chunks + delay * (length - 1))
+    def _(t):
+        slot(t)
+
+    @pl.when(here < length - 1)
+    def _():
+        @pl.loop(0, chunks)
+        def _(c):
+            onward(c).wait_send()
 
 
 def emit_kernel(
@@ -248,7 +335,7 @@
     spread = head_spread(head_count, inner_dim)
     held = (entering[0] + before[0, 0:1] * incoming[...]).astype(BF16)
     carried = jnp.dot(bc[:, state_dim:], held, preferred_element_type=F32)
-    response = y[...] + over_channels(jnp.exp(cum[...]), spread) * carried
+    response = y[...].astype(F32) + over_channels(jnp.exp(cum[...]), spread) * carried
     gated = response * silu(gate[...].astype(F32))
     squares = lax.dot_general(
         (gated * gated).astype(BF16), spread, (((1,), (1,)), ((), ())),
@@ -288,26 +375,6 @@
 
 def struct(shape, dtype):
     return jax.ShapeDtypeStruct(shape, dtype)
-
-
-def earlier_spans(state, factor):
-    length, here = (lax.axis_size("tm"), lax.axis_index("tm"))
-    size = state.shape[1]
-    total, fade = (jnp.zeros_like(state), jnp.ones_like(factor))
-    distance = 1
-    while distance < length:
-        own = state + factor * total
-        own_fade = factor * fade
-        high = own_fade.astype(BF16)
-        low = (own_fade - high.astype(F32)).astype(BF16)
-        packed = jnp.concatenate([own.astype(BF16), high, low], axis=1)
-        got = passed_along(packed, "tm", distance).astype(F32)
-        reached = here >= distance
-        got_fade = jnp.where(reached, got[:, size : size + 1] + got[:, size + 1 : size + 2], 1.0)
-        total = total + fade * got[:, :size]
-        fade = fade * got_fade
-        distance *= 2
-    return total
 
 
 def per_device(
@@ -415,7 +482,7 @@
         name="project",
     )(place[..., None], fetched, norm_gain[None], in_weight)
     edge = passed_along(conv[:, events - 8 :], "tm", 1)
-    x, bc, steps, cum, entering, before, final, factor = pl.pallas_call(
+    xs, bc, cum, entering, before, final, factor = pl.pallas_call(
         lambda *refs: state_kernel(inner_dim, *refs),
         grid=(user_count, blocks),
         in_specs=[
@@ -433,7 +500,6 @@
             rows_of(inner_dim),
             rows_of(2 * state_dim),
             rows_of(head_count),
-            rows_of(head_count),
             one_of(state_dim, inner_dim),
             one_of(8, inner_dim),
             user_of(state_dim, inner_dim),
@@ -442,7 +508,6 @@
         out_shape=[
             struct((user_count, events, inner_dim), BF16),
             struct((user_count, events, 2 * state_dim), BF16),
-            struct((user_count, events, head_count), F32),
             struct((user_count, events, head_count), F32),
             struct((user_count, blocks, state_dim, inner_dim), F32),
             struct((user_count, blocks, 8, inner_dim), F32),
@@ -461,19 +526,30 @@
         conv, step, event_gap[..., None], alive_column, edge,
         conv_weight, conv_bias[None], dt_bias[None], decay_rate[None],
     )
-    incoming = earlier_spans(final, factor[:, 0:1])
-    y = pl.pallas_call(
-        local_kernel,
-        grid=(user_count, blocks),
-        in_specs=[
-            rows_of(inner_dim), rows_of(2 * state_dim), rows_of(head_count), rows_of(head_count),
-        ],
-        out_specs=rows_of(inner_dim),
-        out_shape=struct((user_count, events, inner_dim), F32),
-        compiler_params=params(),
-        cost_estimate=cost(8 << 30, 5 << 20, events * BLOCK * head_count),
+    chunks = user_count * (head_count // 2)
+    pair_width = 2 * (inner_dim // head_count)
+    y, incoming = pl.pallas_call(
+        lambda *refs: local_kernel(head_count, *refs),
+        in_specs=[pl.BlockSpec(memory_space=pltpu.VMEM)] * 5,
+        out_specs=[pl.BlockSpec(memory_space=pltpu.VMEM)] * 2,
+        out_shape=[
+            struct((user_count, events, inner_dim), BF16),
+            struct((user_count, state_dim, inner_dim), F32),
+        ],
+        scratch_shapes=[
+            pltpu.VMEM((user_count * blocks, BLOCK, BLOCK), F32),
+            pltpu.VMEM((user_count * blocks, head_count, BLOCK), F32),
+            pltpu.VMEM((chunks, state_dim, pair_width), BF16),
+            pltpu.VMEM((chunks, state_dim, pair_width), BF16),
+            pltpu.SemaphoreType.DMA((chunks,)),
+            pltpu.SemaphoreType.DMA((chunks,)),
+        ],
+        compiler_params=pltpu.CompilerParams(
+            vmem_limit_bytes=VMEM_LIMIT, collective_id=1, has_side_effects=True
+        ),
+        cost_estimate=cost(8 << 30, 8 << 20, user_count * events * BLOCK * head_count),
         name="local",
-    )(x, bc, steps, cum)
+    )(xs, bc, cum, final, factor)
     return (
         pl.pallas_call(
             emit_kernel,

time: 203 us -> 181 us (0.89)
  Pallas kernels: 129 us -> 153 us
  waiting for transfers between devices: 25.6 us -> 4.29 us
  local copies, waits for them, and re-layouts: 29.7 us -> 15.3 us
  other arithmetic: 7.2 us -> 2.11 us
  starting transfers between devices: 6.39 us -> 1.91 us
    pallas_call x1, Pallas kernels: 8.39 us -> 36 us  [per_device(): pl.pallas_call(lambda *refs: local_kernel(head_count, *refs), in_specs=[p...]
    ppermute x4 -> x1, waiting for transfers between devices: 25.6 us -> 4.29 us  [passed_along(): return lax.ppermute(block, axis, route)]
    unnamed x67 -> x38, local copies, waits for them, and re-layouts: 24.8 us -> 12.3 us
    ppermute x4 -> x1, starting transfers between devices: 6.39 us -> 1.91 us  [passed_along(): return lax.ppermute(block, axis, route)]
    convert_element_type x9 -> x0, other arithmetic: 3.39 us -> none  [the longest x2 2.02 us: earlier_spans(): got = passed_along(packed, 'tm', distance).astype(F32)]
    pallas_call x1, Pallas kernels: 15.2 us -> 12.9 us  [per_device(): pl.pallas_call(lambda *refs: state_kernel(inner_dim, *refs), grid=(user_c...]
  transfers between devices with their start and end apart: 4 -> 1, of which waited for: 4 -> 1; matrix products, arithmetic and copies ran while one was open for 1% -> 0% of each run, Pallas kernels for 4% -> 0%
where the time goes in v3:
time: 181 us; the launch traced here: 178 us
  Pallas kernels  153 us (85%)
  local copies, waits for them, and re-layouts  15.3 us (8%)
  waiting for transfers between devices  4.29 us (2%)
  other arithmetic  2.11 us (1%)
  starting transfers between devices  1.91 us (1%)
    pallas_call x1, Pallas kernels, per_device(): pl.pallas_call(lambda *refs: exchange_kernel(devices, group, *refs), in_s...  82 us
    pallas_call x1, Pallas kernels, per_device(): pl.pallas_call(lambda *refs: local_kernel(head_count, *refs), in_specs=[p...  36 us
    pallas_call x1, Pallas kernels, per_device(): pl.pallas_call(lambda *refs: state_kernel(inner_dim, *refs), grid=(user_c...  12.9 us
    pallas_call x1, Pallas kernels, per_device(): pl.pallas_call(emit_kernel, grid=(user_count, blocks), in_specs=[rows_of(...  12.7 us
    unnamed x38, local copies, waits for them, and re-layouts  12.3 us
    pallas_call x1, Pallas kernels, per_device(): pl.pallas_call(lambda *refs: project_kernel(inner_dim, conv_dim, *refs),...  9.82 us
    ppermute x1, waiting for transfers between devices, passed_along(): return lax.ppermute(block, axis, route)  4.29 us
  transfers between devices with their start and end apart: 1, of which 1 were waited for; matrix products, arithmetic and copies ran while one was open for 0% of the time, Pallas kernels for 0%

profile of v3, /device:TPU:26, one launch (start us, length us, event | category | flops | bytes accessed | tf_op | source)
XLA Modules:
  0.0 178.0 jit_solution(11998653883721611206)
XLA Ops:
  0.0 0.7 copy.46
  0.7 0.4 fusion.9
  1.1 0.7 broadcast_compare_fusion
  1.8 0.7 multiply_subtract_fusion
  2.5 0.4 copy.37
  3.0 0.2 convolution_bitcast_fusion
  3.2 0.1 fusion.20
  3.3 0.1 reshape.68
  3.4 0.3 copy.34
  3.7 1.2 copy.39
  4.9 2.8 %copy.41.refs_3_ = bf16[512,2192]{1,0:T(8,128)(2,1)S(1)} copy(bf16[512,2192]{0,1:T(8,128)(2,1)} %param.19) | data formatting | bytes 4489216 | tf_op args[6]
  7.7 0.0 copy-start.1
  7.7 2.2 %copy-done.1 = bf16[4096,512]{1,0:T(8,128)(2,1)S(1)} copy-done((bf16[4096,512]{1,0:T(8,128)(2,1)S(1)}, bf16[4096,512]{1,0:T(8,128)(2,1)}, u32[]{:S(2)}) %copy-start.1) | copy-done | bytes 4194328
  9.9 0.0 copy-start.14
  9.9 82.0 %exchange.1 = bf16[2,32,48,512]{3,2,1,0:T(8,128)(2,1)S(1)} custom-call(s32[32,1,128]{2,1,0:T(1,128)S(1)} %pad.4.refs_0_, bf16[4096,512]{1,0:T(8,128)(2,1)S(1)} %copy-done.1), custom_call_target="tpu_custom_call" | custom-call | flops 13958643712 | bytes 10485760 | tf_op jit(solution)/shard_map/exchange/pallas_call | solution.py:436
  92.0 0.0 copy-done.14
  92.0 0.0 copy-start.5
  92.0 0.4 fusion.14.refs_0_
  92.4 0.3 copy-done.5
  92.7 0.0 copy-start.17
  92.7 0.0 copy-start.15
  92.7 0.0 copy-start.16
  92.7 0.0 copy-start.3
  92.7 0.0 copy-start.6
  92.7 0.0 copy-start.7
  92.7 9.8 %project.1 = (bf16[2,768,512]{2,1,0:T(8,128)(2,1)S(1)}, bf16[2,768,1024]{2,1,0:T(8,128)(2,1)S(1)}, bf16[2,768,1152]{2,1,0:T(8,128)(2,1)}, f32[2,768,16]{2,1,0:T(8,128)S(1)}) custom-call(s32[2,768,1]{2,1,0:T(8,128)S(1)} %fusion.14.refs_0_, bf16[2,1536,512]{2,1,0:T(8,128)(2,1)S(1)} %bitcast.32, f32[1,512]{1,0:T(1,128)S(1)} %bitcast.29, ...), custom_call_target="tpu_custom_call" | custom-call | flops 2931818496 | bytes 9437184 | tf_op jit(solution)/shard_map/project/pallas_call | solution.py:464
  102.5 0.0 copy-start.8
  102.5 1.7 copy-done.8
  104.2 0.0 copy-start.10
  104.2 1.1 copy-done.10
  105.3 0.8 slice.11
  106.1 1.9 %collective-permute-start = (bf16[2,8,1152]{2,1,0:T(8,128)(2,1)S(1)}, bf16[2,8,1152]{2,1,0:T(8,128)(2,1)S(1)}, u32[]{:S(2)}, u32[]{:S(2)}) collective-permute-start(bf16[2,8,1152]{2,1,0:T(8,128)(2,1)S(1)} %slice.11), channel_id=1, source_target_pairs={{0,4},{4,8},{8,12},{12,16},{16,20},{20,24},{24,28},{1,5},{5,9},{9,... | collective-permute-start | bytes 110600 | tf_op jit(solution)/shard_map/ppermute | solution.py:17
  108.0 0.0 copy-done.17
  108.1 0.2 compare_convert_fusion.refs_3_.alive
  108.2 0.0 copy-done.15
  108.3 0.0 copy-done.16
  108.3 0.3 copy.42.refs_2_
  108.6 4.3 %collective-permute-done.refs_4_ = bf16[2,8,1152]{2,1,0:T(8,128)(2,1)S(1)} collective-permute-done((bf16[2,8,1152]{2,1,0:T(8,128)(2,1)S(1)}, bf16[2,8,1152]{2,1,0:T(8,128)(2,1)S(1)}, u32[]{:S(2)}, u32[]{:S(2)}) %collective-permute-start) | collective-permute-done | bytes 36896 | tf_op jit(solution)/shard_map/ppermute | solution.py:17
  112.9 0.0 copy-done.3
  112.9 0.0 copy-done.6
  112.9 0.0 copy-done.7
  112.9 0.0 copy-start
  112.9 2.0 %copy-done = bf16[2,768,1152]{2,1,0:T(8,128)(2,1)S(1)} copy-done((bf16[2,768,1152]{2,1,0:T(8,128)(2,1)S(1)}, bf16[2,768,1152]{2,1,0:T(8,128)(2,1)}, u32[]{:S(2)}) %copy-start) | copy-done | bytes 3538968
  114.9 12.9 %states.1 = (bf16[2,768,1024]{2,1,0:T(8,128)(2,1)S(1)}, bf16[2,768,128]{2,1,0:T(8,128)(2,1)S(1)}, f32[2,768,16]{2,1,0:T(8,128)S(1)}, f32[2,3,64,1024]{3,2,1,0:T(...) custom-call(bf16[2,768,1152]{2,1,0:T(8,128)(2,1)S(1)} %copy-done, ...), custom_call_target="tpu_custom_call" | custom-call | flops 4294967296 | bytes 8388608 | tf_op jit(solution)/shard_map/states/pallas_call | solution.py:485
  127.8 0.0 copy-start.12
  127.8 0.0 copy-start.2
  127.8 0.0 copy-start.4
  127.8 0.0 copy-start.9
  127.8 0.0 copy-start.11
  127.8 36.0 %local.1 = (bf16[2,768,1024]{2,1,0:T(8,128)(2,1)S(1)}, f32[2,64,1024]{2,1,0:T(8,128)S(1)}) custom-call(bf16[2,768,1024]{2,1,0:T(8,128)(2,1)S(1)} %get-tuple-element.20.refs_0_, bf16[2,768,128]{2,1,0:T(8,128)(2,1)S(1)} %get-tuple-element.21.refs_1_.bc, f32[2,768,16]{2,1,0:T(8,128)S(1)} %get-tuple-element.22.refs_2_.cum, ...), custom_call_target="tpu_custom_call" | custom-call | flops 8589934592 | bytes 8388608 | tf_op jit(solution)/shard_map/local/pallas_call | solution.py:531
  163.8 0.0 copy-done.12
  163.8 0.0 copy-done.2
  163.8 0.0 copy-done.4
  163.8 0.0 copy-done.9
  163.9 0.0 copy-done.11
  163.9 0.0 copy-start.13
  163.9 1.4 copy-done.13
  165.3 12.7 %emit.1 = bf16[2,768,512]{2,1,0:T(8,128)(2,1)} custom-call(bf16[2,768,1024]{2,1,0:T(8,128)(2,1)S(1)} %get-tuple-element.25.y, bf16[2,768,128]{2,1,0:T(8,128)(2,1)S(1)} %get-tuple-element.21.refs_1_.bc, f32[2,768,16]{2,1,0:T(8,128)S(1)} %get-tuple-element.22.refs_2_.cum, bf16[2,768,1024]{2,1,0:T(8,128)(2,1)S(1)} %copy-done.9, ...), custom_call_target="tpu_custom_call" | custom-call | flops 4294967296 | bytes 9437184 | tf_op jit(solution)/shard_map/emit/pallas_call | solution.py:554
  (6 shorter events, 0.1 us)
Async XLA Ops:
  7.7 2.2 %copy-start.1 = (bf16[4096,512]{1,0:T(8,128)(2,1)S(1)}, bf16[4096,512]{1,0:T(8,128)(2,1)}, u32[]{:S(2)}) copy-start(bf16[4096,512]{1,0:T(8,128)(2,1)} %refs_1_.1) | copy-start | bytes 12582916
  9.9 82.1 %copy-start.14 = (s32[2,768,1]{2,1,0:T(8,128)S(1)}, s32[2,768,1]{2,1,0:T(8,128)}, u32[]{:S(2)}) copy-start(s32[2,768,1]{2,1,0:T(8,128)} %copy.39) | copy-start | bytes 18436
  92.0 0.7 copy-start.5
  92.7 15.4 %copy-start.17 = (s32[2]{0:T(128)S(1)}, s32[2]{0:T(128)}, u32[]{:S(2)}) copy-start(s32[2]{0:T(128)} %param.15) | copy-start | bytes 28
  92.7 15.6 %copy-start.15 = (f32[1152]{0:T(1024)S(1)}, f32[1152]{0:T(1024)}, u32[]{:S(2)}) copy-start(f32[1152]{0:T(1024)} %param.21) | copy-start | bytes 13828
  92.7 15.6 %copy-start.16 = (f32[2,768]{1,0:T(2,128)S(1)}, f32[2,768]{1,0:T(2,128)}, u32[]{:S(2)}) copy-start(f32[2,768]{1,0:T(2,128)} %param.16) | copy-start | bytes 18436
  92.7 20.2 %copy-start.3 = (f32[4,1152]{1,0:T(4,128)S(1)}, f32[4,1152]{1,0:T(4,128)}, u32[]{:S(2)}) copy-start(f32[4,1152]{1,0:T(4,128)} %refs_5_.1) | copy-start | bytes 55300
  92.7 20.2 %copy-start.6 = (f32[16]{0:T(128)S(1)}, f32[16]{0:T(128)}, u32[]{:S(2)}) copy-start(f32[16]{0:T(128)} %param.22) | copy-start | bytes 196
  92.7 20.2 %copy-start.7 = (f32[16]{0:T(128)S(1)}, f32[16]{0:T(128)}, u32[]{:S(2)}) copy-start(f32[16]{0:T(128)} %param.23) | copy-start | bytes 196
  102.5 1.7 copy-start.8
  104.2 1.1 copy-start.10
  106.1 6.7 %collective-permute-start = (bf16[2,8,1152]{2,1,0:T(8,128)(2,1)S(1)}, bf16[2,8,1152]{2,1,0:T(8,128)(2,1)S(1)}, u32[]{:S(2)}, u32[]{:S(2)}) collective-permute-start(bf16[2,8,1152]{2,1,0:T(8,128)(2,1)S(1)} %slice.11), channel_id=1, source_target_pairs={{0,4},{4,8},{8,12},{12,16},{16,20},{20,24},{24,28},{1,5},{5,9},{9,... | collective-permute-start | bytes 110600 | tf_op jit(solution)/shard_map/ppermute | solution.py:17
  112.9 2.0 %copy-start = (bf16[2,768,1152]{2,1,0:T(8,128)(2,1)S(1)}, bf16[2,768,1152]{2,1,0:T(8,128)(2,1)}, u32[]{:S(2)}) copy-start(bf16[2,768,1152]{2,1,0:T(8,128)(2,1)} %get-tuple-element.18.refs_0_) | copy-start | bytes 10616836
  127.8 36.1 %copy-start.12 = (f32[2,3,64,1024]{3,2,1,0:T(8,128)}, f32[2,3,64,1024]{3,2,1,0:T(8,128)S(1)}, u32[]{:S(2)}) copy-start(f32[2,3,64,1024]{3,2,1,0:T(8,128)S(1)} %get-tuple-element.28.entering) | copy-start | bytes 4718596
  127.8 36.1 %copy-start.2 = (bf16[1024,512]{1,0:T(8,128)(2,1)S(1)}, bf16[1024,512]{1,0:T(8,128)(2,1)}, u32[]{:S(2)}) copy-start(bf16[1024,512]{1,0:T(8,128)(2,1)} %weight.1) | copy-start | bytes 3145732
  127.8 36.1 %copy-start.4 = (f32[1024]{0:T(1024)S(1)}, f32[1024]{0:T(1024)}, u32[]{:S(2)}) copy-start(f32[1024]{0:T(1024)} %param.24) | copy-start | bytes 12292
  127.8 36.1 %copy-start.9 = (bf16[2,768,1024]{2,1,0:T(8,128)(2,1)S(1)}, bf16[2,768,1024]{2,1,0:T(8,128)(2,1)}, u32[]{:S(2)}) copy-start(bf16[2,768,1024]{2,1,0:T(8,128)(2,1)} %copy-done.8) | copy-start | bytes 9437188
  127.8 36.1 %copy-start.11 = (bf16[2,768,512]{2,1,0:T(8,128)(2,1)S(1)}, bf16[2,768,512]{2,1,0:T(8,128)(2,1)}, u32[]{:S(2)}) copy-start(bf16[2,768,512]{2,1,0:T(8,128)(2,1)} %copy-done.10) | copy-start | bytes 4718596
  163.9 1.4 copy-start.13

commit v4 on v3

--- a/solution.py
+++ b/solution.py
@@ -221,7 +221,7 @@
     width = 2 * (inner_dim // head_count)
     pairs = head_count // 2
     chunks = users * pairs
-    delay = 2
+    delay = 4
 
     barrier = pltpu.get_barrier_semaphore()
 
@@ -301,9 +301,7 @@
         def _(r, pair=pair, lanes=lanes):
             user = r // blocks
 
-            @pl.when(r % blocks == 0)
-            def _():
-                slot(pair * users + user)
+            slot(pair * users * blocks + r)
 
             rows = pl.ds(pl.multiple_of((r % blocks) * BLOCK, BLOCK), BLOCK)
             values = xs[user, rows, lanes]
@@ -315,9 +313,13 @@
                 parts.append(jnp.dot(mixing, values, preferred_element_type=F32))
             y[user, rows, lanes] = jnp.where(left, parts[0], parts[1]).astype(BF16)
 
-    @pl.loop(chunks, chunks + delay * (length - 1))
-    def _(t):
-        slot(t)
+    done = pairs * users * blocks
+    last = chunks + delay * (length - 1)
+    if last > done:
+
+        @pl.loop(done, last)
+        def _(t):
+            slot(t)
 
     @pl.when(here < length - 1)
     def _():

time: 181 us -> 173 us (0.956)
  Pallas kernels: 153 us -> 146 us
    pallas_call x1, Pallas kernels: 36 us -> 28.2 us  [per_device(): pl.pallas_call(lambda *refs: local_kernel(head_count, *refs), in_specs=[p...]
where the time goes in v4:
time: 173 us; the launch traced here: 170 us
  Pallas kernels  146 us (84%)
  local copies, waits for them, and re-layouts  15.3 us (9%)
  waiting for transfers between devices  4.29 us (2%)
  other arithmetic  2.11 us (1%)
  starting transfers between devices  1.91 us (1%)
    pallas_call x1, Pallas kernels, per_device(): pl.pallas_call(lambda *refs: exchange_kernel(devices, group, *refs), in_s...  82 us
    pallas_call x1, Pallas kernels, per_device(): pl.pallas_call(lambda *refs: local_kernel(head_count, *refs), in_specs=[p...  28.2 us
    pallas_call x1, Pallas kernels, per_device(): pl.pallas_call(lambda *refs: state_kernel(inner_dim, *refs), grid=(user_c...  12.9 us
    pallas_call x1, Pallas kernels, per_device(): pl.pallas_call(emit_kernel, grid=(user_count, blocks), in_specs=[rows_of(...  12.7 us
    unnamed x38, local copies, waits for them, and re-layouts  12.3 us
    pallas_call x1, Pallas kernels, per_device(): pl.pallas_call(lambda *refs: project_kernel(inner_dim, conv_dim, *refs),...  9.82 us
    ppermute x1, waiting for transfers between devices, passed_along(): return lax.ppermute(block, axis, route)  4.29 us
  transfers between devices with their start and end apart: 1, of which 1 were waited for; matrix products, arithmetic and copies ran while one was open for 0% of the time, Pallas kernels for 0%

profile of v4, /device:TPU:26, one launch (start us, length us, event | category | flops | bytes accessed | tf_op | source)
XLA Modules:
  0.0 170.2 jit_solution(14772478195758804565)
XLA Ops:
  0.0 0.7 copy.46
  0.7 0.4 fusion.9
  1.1 0.7 broadcast_compare_fusion
  1.8 0.7 multiply_subtract_fusion
  2.5 0.4 copy.37
  3.0 0.2 convolution_bitcast_fusion
  3.2 0.1 fusion.20
  3.3 0.1 reshape.68
  3.4 0.3 copy.34
  3.7 1.2 copy.39
  4.9 2.8 %copy.41.refs_3_ = bf16[512,2192]{1,0:T(8,128)(2,1)S(1)} copy(bf16[512,2192]{0,1:T(8,128)(2,1)} %param.19) | data formatting | bytes 4489216 | tf_op args[6]
  7.7 0.0 copy-start.1
  7.7 2.2 %copy-done.1 = bf16[4096,512]{1,0:T(8,128)(2,1)S(1)} copy-done((bf16[4096,512]{1,0:T(8,128)(2,1)S(1)}, bf16[4096,512]{1,0:T(8,128)(2,1)}, u32[]{:S(2)}) %copy-start.1) | copy-done | bytes 4194328
  9.9 0.0 copy-start.14
  9.9 82.0 %exchange.1 = bf16[2,32,48,512]{3,2,1,0:T(8,128)(2,1)S(1)} custom-call(s32[32,1,128]{2,1,0:T(1,128)S(1)} %pad.4.refs_0_, bf16[4096,512]{1,0:T(8,128)(2,1)S(1)} %copy-done.1), custom_call_target="tpu_custom_call" | custom-call | flops 13958643712 | bytes 10485760 | tf_op jit(solution)/shard_map/exchange/pallas_call | solution.py:438
  92.0 0.0 copy-done.14
  92.0 0.0 copy-start.5
  92.0 0.4 fusion.14.refs_0_
  92.4 0.3 copy-done.5
  92.7 0.0 copy-start.17
  92.7 0.0 copy-start.15
  92.7 0.0 copy-start.16
  92.7 0.0 copy-start.3
  92.7 0.0 copy-start.6
  92.7 0.0 copy-start.7
  92.7 9.8 %project.1 = (bf16[2,768,512]{2,1,0:T(8,128)(2,1)S(1)}, bf16[2,768,1024]{2,1,0:T(8,128)(2,1)S(1)}, bf16[2,768,1152]{2,1,0:T(8,128)(2,1)}, f32[2,768,16]{2,1,0:T(8,128)S(1)}) custom-call(s32[2,768,1]{2,1,0:T(8,128)S(1)} %fusion.14.refs_0_, bf16[2,1536,512]{2,1,0:T(8,128)(2,1)S(1)} %bitcast.32, f32[1,512]{1,0:T(1,128)S(1)} %bitcast.29, ...), custom_call_target="tpu_custom_call" | custom-call | flops 2931818496 | bytes 9437184 | tf_op jit(solution)/shard_map/project/pallas_call | solution.py:466
  102.5 0.0 copy-start.8
  102.5 1.7 copy-done.8
  104.2 0.0 copy-start.10
  104.2 1.1 copy-done.10
  105.3 0.8 slice.11
  106.1 1.9 %collective-permute-start = (bf16[2,8,1152]{2,1,0:T(8,128)(2,1)S(1)}, bf16[2,8,1152]{2,1,0:T(8,128)(2,1)S(1)}, u32[]{:S(2)}, u32[]{:S(2)}) collective-permute-start(bf16[2,8,1152]{2,1,0:T(8,128)(2,1)S(1)} %slice.11), channel_id=1, source_target_pairs={{0,4},{4,8},{8,12},{12,16},{16,20},{20,24},{24,28},{1,5},{5,9},{9,... | collective-permute-start | bytes 110600 | tf_op jit(solution)/shard_map/ppermute | solution.py:17
  108.0 0.0 copy-done.17
  108.1 0.2 compare_convert_fusion.refs_3_.alive
  108.2 0.0 copy-done.15
  108.3 0.0 copy-done.16
  108.3 0.3 copy.42.refs_2_
  108.6 4.3 %collective-permute-done.refs_4_ = bf16[2,8,1152]{2,1,0:T(8,128)(2,1)S(1)} collective-permute-done((bf16[2,8,1152]{2,1,0:T(8,128)(2,1)S(1)}, bf16[2,8,1152]{2,1,0:T(8,128)(2,1)S(1)}, u32[]{:S(2)}, u32[]{:S(2)}) %collective-permute-start) | collective-permute-done | bytes 36896 | tf_op jit(solution)/shard_map/ppermute | solution.py:17
  112.9 0.0 copy-done.3
  112.9 0.0 copy-done.6
  112.9 0.0 copy-done.7
  112.9 0.0 copy-start
  112.9 2.0 %copy-done = bf16[2,768,1152]{2,1,0:T(8,128)(2,1)S(1)} copy-done((bf16[2,768,1152]{2,1,0:T(8,128)(2,1)S(1)}, bf16[2,768,1152]{2,1,0:T(8,128)(2,1)}, u32[]{:S(2)}) %copy-start) | copy-done | bytes 3538968
  114.9 12.9 %states.1 = (bf16[2,768,1024]{2,1,0:T(8,128)(2,1)S(1)}, bf16[2,768,128]{2,1,0:T(8,128)(2,1)S(1)}, f32[2,768,16]{2,1,0:T(8,128)S(1)}, f32[2,3,64,1024]{3,2,1,0:T(...) custom-call(bf16[2,768,1152]{2,1,0:T(8,128)(2,1)S(1)} %copy-done, ...), custom_call_target="tpu_custom_call" | custom-call | flops 4294967296 | bytes 8388608 | tf_op jit(solution)/shard_map/states/pallas_call | solution.py:487
  127.8 0.0 copy-start.12
  127.8 0.0 copy-start.2
  127.8 0.0 copy-start.4
  127.8 0.0 copy-start.9
  127.8 0.0 copy-start.11
  127.8 28.2 %local.1 = (bf16[2,768,1024]{2,1,0:T(8,128)(2,1)S(1)}, f32[2,64,1024]{2,1,0:T(8,128)S(1)}) custom-call(bf16[2,768,1024]{2,1,0:T(8,128)(2,1)S(1)} %get-tuple-element.20.refs_0_, bf16[2,768,128]{2,1,0:T(8,128)(2,1)S(1)} %get-tuple-element.21.refs_1_.bc, f32[2,768,16]{2,1,0:T(8,128)S(1)} %get-tuple-element.22.refs_2_.cum, ...), custom_call_target="tpu_custom_call" | custom-call | flops 8589934592 | bytes 8388608 | tf_op jit(solution)/shard_map/local/pallas_call | solution.py:533
  156.0 0.0 copy-done.12
  156.0 0.0 copy-done.2
  156.0 0.0 copy-done.4
  156.1 0.0 copy-done.9
  156.1 0.0 copy-done.11
  156.1 0.0 copy-start.13
  156.1 1.4 copy-done.13
  157.5 12.7 %emit.1 = bf16[2,768,512]{2,1,0:T(8,128)(2,1)} custom-call(bf16[2,768,1024]{2,1,0:T(8,128)(2,1)S(1)} %get-tuple-element.25.y, bf16[2,768,128]{2,1,0:T(8,128)(2,1)S(1)} %get-tuple-element.21.refs_1_.bc, f32[2,768,16]{2,1,0:T(8,128)S(1)} %get-tuple-element.22.refs_2_.cum, bf16[2,768,1024]{2,1,0:T(8,128)(2,1)S(1)} %copy-done.9, ...), custom_call_target="tpu_custom_call" | custom-call | flops 4294967296 | bytes 9437184 | tf_op jit(solution)/shard_map/emit/pallas_call | solution.py:556
  (6 shorter events, 0.1 us)
Async XLA Ops:
  7.7 2.2 %copy-start.1 = (bf16[4096,512]{1,0:T(8,128)(2,1)S(1)}, bf16[4096,512]{1,0:T(8,128)(2,1)}, u32[]{:S(2)}) copy-start(bf16[4096,512]{1,0:T(8,128)(2,1)} %refs_1_.1) | copy-start | bytes 12582916
  9.9 82.1 %copy-start.14 = (s32[2,768,1]{2,1,0:T(8,128)S(1)}, s32[2,768,1]{2,1,0:T(8,128)}, u32[]{:S(2)}) copy-start(s32[2,768,1]{2,1,0:T(8,128)} %copy.39) | copy-start | bytes 18436
  92.0 0.7 copy-start.5
  92.7 15.4 %copy-start.17 = (s32[2]{0:T(128)S(1)}, s32[2]{0:T(128)}, u32[]{:S(2)}) copy-start(s32[2]{0:T(128)} %param.15) | copy-start | bytes 28
  92.7 15.6 %copy-start.15 = (f32[1152]{0:T(1024)S(1)}, f32[1152]{0:T(1024)}, u32[]{:S(2)}) copy-start(f32[1152]{0:T(1024)} %param.21) | copy-start | bytes 13828
  92.7 15.6 %copy-start.16 = (f32[2,768]{1,0:T(2,128)S(1)}, f32[2,768]{1,0:T(2,128)}, u32[]{:S(2)}) copy-start(f32[2,768]{1,0:T(2,128)} %param.16) | copy-start | bytes 18436
  92.7 20.2 %copy-start.3 = (f32[4,1152]{1,0:T(4,128)S(1)}, f32[4,1152]{1,0:T(4,128)}, u32[]{:S(2)}) copy-start(f32[4,1152]{1,0:T(4,128)} %refs_5_.1) | copy-start | bytes 55300
  92.7 20.2 %copy-start.6 = (f32[16]{0:T(128)S(1)}, f32[16]{0:T(128)}, u32[]{:S(2)}) copy-start(f32[16]{0:T(128)} %param.22) | copy-start | bytes 196
  92.7 20.2 %copy-start.7 = (f32[16]{0:T(128)S(1)}, f32[16]{0:T(128)}, u32[]{:S(2)}) copy-start(f32[16]{0:T(128)} %param.23) | copy-start | bytes 196
  102.5 1.7 copy-start.8
  104.2 1.1 copy-start.10
  106.1 6.7 %collective-permute-start = (bf16[2,8,1152]{2,1,0:T(8,128)(2,1)S(1)}, bf16[2,8,1152]{2,1,0:T(8,128)(2,1)S(1)}, u32[]{:S(2)}, u32[]{:S(2)}) collective-permute-start(bf16[2,8,1152]{2,1,0:T(8,128)(2,1)S(1)} %slice.11), channel_id=1, source_target_pairs={{0,4},{4,8},{8,12},{12,16},{16,20},{20,24},{24,28},{1,5},{5,9},{9,... | collective-permute-start | bytes 110600 | tf_op jit(solution)/shard_map/ppermute | solution.py:17
  112.9 2.0 %copy-start = (bf16[2,768,1152]{2,1,0:T(8,128)(2,1)S(1)}, bf16[2,768,1152]{2,1,0:T(8,128)(2,1)}, u32[]{:S(2)}) copy-start(bf16[2,768,1152]{2,1,0:T(8,128)(2,1)} %get-tuple-element.18.refs_0_) | copy-start | bytes 10616836
  127.8 28.3 %copy-start.12 = (f32[2,3,64,1024]{3,2,1,0:T(8,128)}, f32[2,3,64,1024]{3,2,1,0:T(8,128)S(1)}, u32[]{:S(2)}) copy-start(f32[2,3,64,1024]{3,2,1,0:T(8,128)S(1)} %get-tuple-element.28.entering) | copy-start | bytes 4718596
  127.8 28.3 %copy-start.2 = (bf16[1024,512]{1,0:T(8,128)(2,1)S(1)}, bf16[1024,512]{1,0:T(8,128)(2,1)}, u32[]{:S(2)}) copy-start(bf16[1024,512]{1,0:T(8,128)(2,1)} %weight.1) | copy-start | bytes 3145732
  127.8 28.3 %copy-start.4 = (f32[1024]{0:T(1024)S(1)}, f32[1024]{0:T(1024)}, u32[]{:S(2)}) copy-start(f32[1024]{0:T(1024)} %param.24) | copy-start | bytes 12292
  127.8 28.3 %copy-start.9 = (bf16[2,768,1024]{2,1,0:T(8,128)(2,1)S(1)}, bf16[2,768,1024]{2,1,0:T(8,128)(2,1)}, u32[]{:S(2)}) copy-start(bf16[2,768,1024]{2,1,0:T(8,128)(2,1)} %copy-done.8) | copy-start | bytes 9437188
  127.8 28.3 %copy-start.11 = (bf16[2,768,512]{2,1,0:T(8,128)(2,1)S(1)}, bf16[2,768,512]{2,1,0:T(8,128)(2,1)}, u32[]{:S(2)}) copy-start(bf16[2,768,512]{2,1,0:T(8,128)(2,1)} %copy-done.10) | copy-start | bytes 4718596
  156.1 1.4 copy-start.13
